TPU v7x, 256 devices: a whole 4x4x8 slice. The times are simulated.
256 devices in a mesh: dp: 32 (over x, y, core), tp: 8 (over z).
Axes of the slice: x: 4, y: 4, z: 8, core: 2. Of those that a mesh axis runs over, the one named last changes fastest.
Arguments:
- hidden_in: bfloat16 [8192, 7168], P('dp', 'tp'), may hold values from -6 to 6
- kv_down: bfloat16 [7168, 576], P('tp'), may hold values from -0.0625 to 0.0625
- latent_gain: float32 [512], replicated, may hold values from 0.5 to 1.5
- q_nope: bfloat16 [8192, 16384], P('dp', 'tp'), may hold values from -6 to 6
- q_rope: bfloat16 [8192, 8192], P('dp', 'tp'), may hold values from -24 to 24
- absorb_k: bfloat16 [128, 128, 512], P('tp'), may hold values from -0.5 to 0.5
- absorb_v: bfloat16 [128, 512, 128], P('tp'), may hold values from -1 to 1
- store: bfloat16 [1536, 64, 576], P('dp'), may hold values from -25 to 25
- page_owner: int32 [64, 16, 1], P('dp'), may hold values from 0 to 31; in each aligned block of 32 rows (0 to 31, 32 to 63, ..., all dimensions but the last counted through in order) at most 2 rows name the same one
- page_slot: int32 [64, 16], P('dp'), may hold values from 0 to 47
- prefix_len: int32 [64], P('dp'), may hold values from 256 to 1024, as said below
Outputs:
- attn_out: bfloat16 [8192, 16384], P('dp', 'tp')
- new_latent: bfloat16 [8192, 576], P('dp')
Inputs may be any that keep to these rules, and one draw needn't show every extreme that they name: `page_owner`: in each aligned block of 32 entries (the requests of one index of dp) no owner is named more than 2 times, and in some block one owner is named exactly 2 times. `prefix_len`: one request at least has a cached prefix of exactly 1024 tokens.
All inputs are finite; a program needn't handle non-finite values.
Results may differ from a plain program's by a relative error of at most 0.0068.
Values may be sent and summed in bfloat16 or wider, within the bound.
No kernel may reach another device: no remote copies, remote signals or barrier semaphores. Data moves between devices by JAX's collectives and lax.ppermute only.
A program may use at most 128 MiB of HBM per device.

v0:
```python
import jax
import jax.numpy as jnp
from jax import lax
from jax.sharding import PartitionSpec as P


def rope_rotate(rotated, position):
    half_width = rotated.shape[-1] // 2
    frequency = 10000.0 ** (-jnp.arange(half_width, dtype=jnp.float32) / half_width)
    angles = position[:, None].astype(jnp.float32) * frequency[None, :]
    cosine = jnp.cos(angles)
    sine_part = jnp.sin(angles)
    first_half = rotated[:, :half_width]
    second_half = rotated[:, half_width:]
    return jnp.concatenate(
        [
            first_half * cosine - second_half * sine_part,
            second_half * cosine + first_half * sine_part,
        ],
        axis=1,
    )


def finish_latent(raw_latent, latent_gain, position):
    width = latent_gain.shape[0]
    compressed = raw_latent[:, :width]
    mean_square = jnp.mean(compressed * compressed, axis=1, keepdims=True)
    normed = compressed * lax.rsqrt(mean_square + 1e-06) * latent_gain[None, :]
    turned = rope_rotate(raw_latent[:, width:], position)
    return jnp.concatenate([normed, turned], axis=1).astype(jnp.bfloat16)


def positions(prefix_len, row_count, new_len):
    token_ids = jnp.arange(row_count, dtype=jnp.int32)
    request_ids = token_ids // new_len
    request_hot = request_ids[:, None] == jnp.arange(prefix_len.shape[0], dtype=jnp.int32)[None, :]
    cached_of = jnp.sum(jnp.where(request_hot, prefix_len[None, :], 0), axis=1)
    return cached_of + token_ids % new_len


def shards(
    hidden_in,
    kv_down,
    latent_gain,
    q_nope,
    q_rope,
    absorb_k,
    absorb_v,
    store,
    page_owner,
    page_slot,
    prefix_len,
):
    tok_dev = hidden_in.shape[0]
    reqs_dev = prefix_len.shape[0]
    new_len = tok_dev // reqs_dev
    kv_rank = latent_gain.shape[0]
    lat_width = kv_down.shape[1]
    heads_dev = absorb_k.shape[0]
    nope_width = absorb_k.shape[1]
    rope_width = q_rope.shape[1] // heads_dev
    vdim_width = absorb_v.shape[2]
    dp_size = lax.axis_size("dp")
    raw_latent = jnp.dot(hidden_in, kv_down, preferred_element_type=jnp.float32)
    raw_latent = lax.psum(raw_latent, "tp")
    new_latent = finish_latent(raw_latent, latent_gain, positions(prefix_len, tok_dev, new_len))
    owners = page_owner.reshape(-1)
    slot_list = page_slot.reshape(-1)
    entries = owners.shape[0]
    capacity = max(2, 2 * ((entries + dp_size - 1) // dp_size))
    row_iota = jnp.arange(entries, dtype=jnp.int32)
    earlier = (owners[:, None] == owners[None, :]) & (row_iota[None, :] < row_iota[:, None])
    rank_within = jnp.sum(earlier.astype(jnp.int32), axis=1)
    owner_hot = owners[:, None] == jnp.arange(dp_size, dtype=jnp.int32)[None, :]
    rank_hot = rank_within[:, None] == jnp.arange(capacity, dtype=jnp.int32)[None, :]
    want_table = (
        jnp.sum(
            jnp.where(
                owner_hot[:, :, None] & rank_hot[:, None, :], slot_list[:, None, None] + 1, 0
            ),
            axis=0,
        )
        - 1
    )
    asked_ids = lax.all_to_all(want_table, "dp", split_axis=0, concat_axis=0, tiled=True)
    asked_ids = jnp.clip(asked_ids, 0, store.shape[0] - 1)
    reply_pages = store[asked_ids]
    fetched = lax.all_to_all(reply_pages, "dp", split_axis=0, concat_axis=0, tiled=True)
    picked = fetched[owners, rank_within]
    cached_keys = picked.reshape(reqs_dev, -1, lat_width)
    cached_cap = cached_keys.shape[1]
    scale = 1.0 / jnp.sqrt(jnp.float32(nope_width + rope_width))

    def attend(inputs):
        query_nope, query_rope, request_keys, new_keys, cached_len = inputs
        q_latent = jnp.einsum(
            "thn,hnc->thc", query_nope, absorb_k, preferred_element_type=jnp.float32
        ).astype(jnp.bfloat16)
        q_full = jnp.concatenate([q_latent, query_rope], axis=2)
        keys = jnp.concatenate([request_keys, new_keys], axis=0)
        scores = jnp.einsum("thc,kc->htk", q_full, keys, preferred_element_type=jnp.float32) * scale
        key_idx = jnp.arange(cached_cap + new_len, dtype=jnp.int32)[None, :]
        tok_idx = jnp.arange(new_len, dtype=jnp.int32)[:, None]
        usable = jnp.where(
            key_idx < cached_cap, key_idx < cached_len, key_idx - cached_cap <= tok_idx
        )
        scores = jnp.where(usable[None], scores, -1e30)
        row_max = jnp.max(scores, axis=2, keepdims=True)
        expo = jnp.exp(scores - row_max)
        total = jnp.sum(expo, axis=2, keepdims=True)
        probs = expo.astype(jnp.bfloat16)
        lat_out = jnp.einsum(
            "htk,kc->thc", probs, keys[:, :kv_rank], preferred_element_type=jnp.float32
        )
        lat_out = (lat_out / jnp.transpose(total, (1, 0, 2))).astype(jnp.bfloat16)
        result = jnp.einsum("thc,hcv->thv", lat_out, absorb_v, preferred_element_type=jnp.float32)
        return result.astype(jnp.bfloat16).reshape(new_len, heads_dev * vdim_width)

    outputs = lax.map(
        attend,
        (
            q_nope.reshape(reqs_dev, new_len, heads_dev, nope_width),
            q_rope.reshape(reqs_dev, new_len, heads_dev, rope_width),
            cached_keys,
            new_latent.reshape(reqs_dev, new_len, lat_width),
            prefix_len,
        ),
    )
    return (outputs.reshape(tok_dev, heads_dev * vdim_width), new_latent)


def solution(mesh):
    placed = (
        P("dp", "tp"),
        P("tp", None),
        P(),
        P("dp", "tp"),
        P("dp", "tp"),
        P("tp", None, None),
        P("tp", None, None),
        P("dp", None, None),
        P("dp", None, None),
        P("dp", None),
        P("dp"),
    )
    return jax.shard_map(
        shards,
        mesh=mesh,
        in_specs=placed,
        out_specs=(P("dp", "tp"), P("dp", None)),
        check_vma=False,
    )
```

profile of v0, /device:TPU:6, one launch (start us, length us, event | category | flops | bytes accessed | tf_op | source)
XLA Modules:
  0.0 192.7 jit_solution(17169045130932891362)
XLA Ops:
  7.7 1.3 reduce.5
  10.3 12.9 %all_to_all.11 = s32[32,1,2]{2,1,0:T(1,128)S(1)} all-to-all(s32[32,1,2]{2,1,0:T(1,128)S(1)} %copy.75), channel_id=1, replica_groups=mesh['dp'=32,'tp'=8] {'dp'}, dimensions={0} | all-to-all | bytes 512 | tf_op jit(solution)/shard_map/all_to_all | solution.py:85
  23.5 5.6 %gather_fusion = bf16[64,64,576]{2,1,0:T(8,128)(2,1)} fusion(bf16[48,64,576]{2,1,0:T(8,128)(2,1)} %param.20, s32[1024]{0:T(1024)S(1)} %pad_clamp_fusion), kind=kCustom, calls=%fused_computation | custom fusion | bytes 9437440 | tf_op jit(solution)/shard_map/gather | solution.py:87
  29.2 6.8 %all-to-all-start.1 = ((bf16[32,2,64,576]{3,2,1,0:T(8,128)(2,1)}), bf16[32,2,64,576]{3,2,1,0:T(8,128)(2,1)}, u32[]{:S(2)}, u32[]{:S(2)}) async-start(bf16[32,2,64,576]{3,2,1,0:T(8,128)(2,1)} %bitcast.124), calls=%async_computation.1 | async-start | bytes 10485760 | tf_op jit(solution)/shard_map/all_to_all | solution.py:88
  36.1 1.4 fusion.57
  37.6 2.6 %copy.99 = bf16[32,8,16,128]{3,2,1,0:T(8,128)(2,1)} copy(bf16[32,8,16,128]{3,1,2,0:T(8,128)(2,1)} %bitcast.129) | data formatting | bytes 2097152
  40.2 2.5 %reshape.286 = bf16[2,128,16,64]{3,2,1,0:T(8,128)(2,1)} reshape(bf16[256,1024]{1,0:T(8,128)(2,1)} %param.17) | data formatting | bytes 1048576 | tf_op jit(solution)/shard_map/reshape | solution.py:123
  42.6 2.6 %copy.85 = bf16[16,512,128]{1,2,0:T(8,128)(2,1)} copy(bf16[16,512,128]{2,1,0:T(8,128)(2,1)S(1)} %copy-done.5) | data formatting | bytes 4194304 | tf_op jit(solution)/shard_map/while | solution.py:119
  45.4 70.5 %all-reduce.2.cloned.1.call-done = f32[256,576]{0,1:T(8,128)} async-done(((f32[256,576]{0,1:T(8,128)}), f32[256,576]{0,1:T(8,128)}) %all-reduce.2.cloned.1.call-update) | async-done | bytes 589840 | tf_op jit(solution)/shard_map/psum | solution.py:65
  115.9 1.1 multiply_reduce_fusion
  118.0 1.2 multiply_convert_fusion
  119.9 1.2 copy_bitcast_fusion.3
  121.8 4.9 %gather_fusion.1 = bf16[32,64,576]{2,1,0:T(8,128)(2,1)} fusion(bf16[32,2,64,576]{3,2,1,0:T(8,128)(2,1)} %all-to-all-done.1, s32[32]{0:T(128)S(1)} %fusion.56), kind=kCustom, calls=%fused_computation.1 | custom fusion | bytes 4718848 | tf_op jit(solution)/shard_map/gather | solution.py:89
  126.7 4.5 %copy.82 = bf16[2,1024,576]{1,2,0:T(8,128)(2,1)} copy(bf16[2,1024,576]{2,1,0:T(8,128)(2,1)} %bitcast.128) | data formatting | bytes 4718592 | tf_op jit(solution)/shard_map/while | solution.py:119
  131.2 54.6 %while.12 = (s32[]{:T(128)}, bf16[2,128,2048]{2,1,0:T(8,128)(2,1)}, bf16[2,1024,576]{1,2,0:T(8,128)(2,1)}, bf16[2,128,576]{1,2,0:T(8,128)(2,1)}, s32[2]{0:T(128)...) while((s32[]{:T(128)}, bf16[2,128,2048]{2,1,0:T(8,128)(2,1)}, ...), condition=%wide.region_8.9_spmd, body=%wide.region_5.8_spmd.sunk | while | flops 5710085632 | bytes 100062952 | solution.py:119
  132.6 1.1 fusion.78
  134.6 1.1 constant_dynamic-slice_fusion.4
  135.8 1.1 constant_dynamic-slice_fusion.5
  137.7 4.2 %fusion.79 = (f32[16,128]{1,0:T(8,128)S(1)}, f32[1152,128,16]{1,0,2:T(8,128)S(1)}) fusion(pred[128,1152]{0,1:T(8,128)(4,1)S(1)} %fusion.78, bf16[128,16,64]{2,0,1:T(8,128)(2,1)S(1)} %bitcast.125, bf16[128,16,512]{2,0,1:T(8,128)(2,1)S(1)} %convert_bitcast_fusion.2, bf16[128,576]{0,1:T(8,128)(2,1)S(1)} %dynamic-slice_bitcast_fusion.4, ...), kind=kOutput, calls=%fused_computation.6.clone.1 | convolution fusion | flops 2732357632 | bytes 13279232 | tf_op jit(solution)/shard_map/while/body/eval_jaxpr/thc,kc->htk/dot_general | solution.py:101
  141.9 1.9 fusion.80
  143.8 1.7 copy-done.1
  145.5 9.0 %fusion.81 = bf16[16,128,128]{1,2,0:T(8,128)(2,1)} fusion(bf16[16,512,128]{1,2,0:T(8,128)(2,1)} %get-tuple-element.287, f32[1152,128,16]{1,0,2:T(8,128)} %copy-done.1, f32[16,128]{1,0:T(8,128)S(1)} %get-tuple-element.258, pred[128,1152]{0,1:T(8,128)(4,1)S(1)} %fusion.78, f32[128,16]{0,1:T(8,128)S(1)} %bitcast.130, bf16[1024,576]{0,1:T(8,128)(2,1)} %copy-done.3, ...), kind=kOutput, calls=%fused_computation.23.clone.1 | convolution fusion | flops 2698510336 | bytes 13549568 | tf_op jit(solution)/shard_map/while/body/eval_jaxpr/thc,hcv->thv/dot_general | solution.py:116
  154.6 2.1 %copy.112 = bf16[1,128,2048]{2,1,0:T(8,128)(2,1)} copy(bf16[1,128,2048]{1,2,0:T(8,128)(2,1)} %bitcast.126) | data formatting | bytes 1048576 | tf_op jit(solution)/shard_map/while/body/jit(dynamic_update_index_in_dim)/dynamic_update_slice | solution.py:119
  156.6 1.9 constant_dynamic-update-slice_fusion.2
  161.9 1.1 constant_dynamic-slice_fusion.4
  163.1 1.1 constant_dynamic-slice_fusion.5
  165.0 4.2 %fusion.79 = (f32[16,128]{1,0:T(8,128)S(1)}, f32[1152,128,16]{1,0,2:T(8,128)S(1)}) fusion(pred[128,1152]{0,1:T(8,128)(4,1)S(1)} %fusion.78, bf16[128,16,64]{2,0,1:T(8,128)(2,1)S(1)} %bitcast.125, bf16[128,16,512]{2,0,1:T(8,128)(2,1)S(1)} %convert_bitcast_fusion.2, bf16[128,576]{0,1:T(8,128)(2,1)S(1)} %dynamic-slice_bitcast_fusion.4, ...), kind=kOutput, calls=%fused_computation.6.clone.1 | convolution fusion | flops 2732357632 | bytes 13279232 | tf_op jit(solution)/shard_map/while/body/eval_jaxpr/thc,kc->htk/dot_general | solution.py:101
  169.2 1.9 fusion.80
  171.1 1.7 copy-done.1
  172.8 9.0 %fusion.81 = bf16[16,128,128]{1,2,0:T(8,128)(2,1)} fusion(bf16[16,512,128]{1,2,0:T(8,128)(2,1)} %get-tuple-element.287, f32[1152,128,16]{1,0,2:T(8,128)} %copy-done.1, f32[16,128]{1,0:T(8,128)S(1)} %get-tuple-element.258, pred[128,1152]{0,1:T(8,128)(4,1)S(1)} %fusion.78, f32[128,16]{0,1:T(8,128)S(1)} %bitcast.130, bf16[1024,576]{0,1:T(8,128)(2,1)} %copy-done.3, ...), kind=kOutput, calls=%fused_computation.23.clone.1 | convolution fusion | flops 2698510336 | bytes 13549568 | tf_op jit(solution)/shard_map/while/body/eval_jaxpr/thc,hcv->thv/dot_general | solution.py:116
  181.9 2.1 %copy.112 = bf16[1,128,2048]{2,1,0:T(8,128)(2,1)} copy(bf16[1,128,2048]{1,2,0:T(8,128)(2,1)} %bitcast.126) | data formatting | bytes 1048576 | tf_op jit(solution)/shard_map/while/body/jit(dynamic_update_index_in_dim)/dynamic_update_slice | solution.py:119
  183.9 1.9 constant_dynamic-update-slice_fusion.2
  (69 shorter events, 12.3 us)
Async XLA Ops:
  7.2 28.9 %copy-start = (bf16[896,576]{0,1:T(8,128)(2,1)S(1)}, bf16[896,576]{0,1:T(8,128)(2,1)}, u32[]{:S(2)}) copy-start(bf16[896,576]{0,1:T(8,128)(2,1)} %param.14) | copy-start | bytes 3096580
  29.2 6.9 %copy-start.6 = (bf16[256,896]{1,0:T(8,128)(2,1)S(1)}, bf16[256,896]{1,0:T(8,128)(2,1)}, u32[]{:S(2)}) copy-start(bf16[256,896]{1,0:T(8,128)(2,1)} %param.13) | copy-start | bytes 1376260
  29.2 92.6 %all-to-all-start.1 = ((bf16[32,2,64,576]{3,2,1,0:T(8,128)(2,1)}), bf16[32,2,64,576]{3,2,1,0:T(8,128)(2,1)}, u32[]{:S(2)}, u32[]{:S(2)}) async-start(bf16[32,2,64,576]{3,2,1,0:T(8,128)(2,1)} %bitcast.124), calls=%async_computation.1 | async-start | bytes 10485760 | tf_op jit(solution)/shard_map/all_to_all | solution.py:88
  36.0 1.5 copy-start.8
  36.0 79.8 %all-reduce.2.cloned.1.call-start = ((), (), s32[]{:S(2)}) async-start(), calls=%async_computation.2 | async-start | bytes 1179648 | tf_op jit(solution)/shard_map/psum | solution.py:65
  37.4 5.2 %copy-start.5 = (bf16[16,512,128]{2,1,0:T(8,128)(2,1)S(1)}, bf16[16,512,128]{2,1,0:T(8,128)(2,1)}, u32[]{:S(2)}) copy-start(bf16[16,512,128]{2,1,0:T(8,128)(2,1)} %param.19) | copy-start | bytes 6291460
  40.2 5.1 %copy-start.9 = (s32[2]{0:T(128)S(1)}, s32[2]{0:T(128)}, u32[]{:S(2)}) copy-start(s32[2]{0:T(128)} %param.23) | copy-start | bytes 28
  42.6 75.3 %copy-start.7 = (f32[512]{0:T(512)S(1)}, f32[512]{0:T(512)}, u32[]{:S(2)}) copy-start(f32[512]{0:T(512)} %param.15) | copy-start | bytes 6148
  126.7 4.5 %copy-start.2 = (bf16[16,128,512]{2,1,0:T(8,128)(2,1)S(1)}, bf16[16,128,512]{2,1,0:T(8,128)(2,1)}, u32[]{:S(2)}) copy-start(bf16[16,128,512]{2,1,0:T(8,128)(2,1)} %param.18) | copy-start | bytes 6291460
  131.2 5.7 %copy-start.4 = (bf16[2,1024,576]{1,2,0:T(8,128)(2,1)S(1)}, bf16[2,1024,576]{1,2,0:T(8,128)(2,1)}, u32[]{:S(2)}) copy-start(bf16[2,1024,576]{1,2,0:T(8,128)(2,1)} %get-tuple-element.281) | copy-start | bytes 7077892 | tf_op jit(solution)/shard_map/while
  137.0 4.9 %copy-start.3 = (bf16[1024,576]{0,1:T(8,128)(2,1)}, bf16[1024,576]{0,1:T(8,128)(2,1)S(1)}, u32[]{:S(2)}) copy-start(bf16[1024,576]{0,1:T(8,128)(2,1)S(1)} %dynamic-slice_bitcast_fusion.5) | copy-start | bytes 3538948 | tf_op jit(solution)/shard_map/while
  141.9 3.6 %copy-start.1 = (f32[1152,128,16]{1,0,2:T(8,128)}, f32[1152,128,16]{1,0,2:T(8,128)S(1)}, u32[]{:S(2)}) copy-start(f32[1152,128,16]{1,0,2:T(8,128)S(1)} %get-tuple-element.257) | copy-start | bytes 28311556 | tf_op jit(solution)/shard_map/while
  158.5 5.7 %copy-start.4 = (bf16[2,1024,576]{1,2,0:T(8,128)(2,1)S(1)}, bf16[2,1024,576]{1,2,0:T(8,128)(2,1)}, u32[]{:S(2)}) copy-start(bf16[2,1024,576]{1,2,0:T(8,128)(2,1)} %get-tuple-element.281) | copy-start | bytes 7077892 | tf_op jit(solution)/shard_map/while
  164.3 4.9 %copy-start.3 = (bf16[1024,576]{0,1:T(8,128)(2,1)}, bf16[1024,576]{0,1:T(8,128)(2,1)S(1)}, u32[]{:S(2)}) copy-start(bf16[1024,576]{0,1:T(8,128)(2,1)S(1)} %dynamic-slice_bitcast_fusion.5) | copy-start | bytes 3538948 | tf_op jit(solution)/shard_map/while
  169.2 3.6 %copy-start.1 = (f32[1152,128,16]{1,0,2:T(8,128)}, f32[1152,128,16]{1,0,2:T(8,128)S(1)}, u32[]{:S(2)}) copy-start(f32[1152,128,16]{1,0,2:T(8,128)S(1)} %get-tuple-element.257) | copy-start | bytes 28311556 | tf_op jit(solution)/shard_map/while
Sparse Core Ops, SparseCore 0:
  39.2 76.6 all-reduce.1
where the time goes:
time: 194 us; the launch traced here: 193 us
  waiting for transfers between devices  70.5 us (36%)
  local copies, waits for them, and re-layouts  43 us (22%)
  matrix products  29.2 us (15%)
  other arithmetic  15.8 us (8%)
  between operations  14.2 us (7%)
  blocking collectives  12.9 us (7%)
  starting transfers between devices  6.86 us (4%)
    psum x1, waiting for transfers between devices, shards(): raw_latent = lax.psum(raw_latent, 'tp')  70.5 us
    dot_general x2, matrix products, attend(): jnp.einsum('thc,hcv->thv', lat_out, absorb_v, preferred_element_type=jnp....  18.1 us
    all_to_all x1, blocking collectives, shards(): lax.all_to_all(want_table, 'dp', split_axis=0, concat_axis=0, tiled=True)  12.9 us
    dot_general x2, matrix products, attend(): jnp.einsum('thc,kc->htk', q_full, keys, preferred_element_type=jnp.float32)  8.37 us
    dynamic_update_slice x4, local copies, waits for them, and re-layouts, shards(): lax.map(attend, (q_nope.reshape(reqs_dev, new_len, heads_dev, nope_width)...  7.88 us
    while x2, local copies, waits for them, and re-layouts, shards(): lax.map(attend, (q_nope.reshape(reqs_dev, new_len, heads_dev, nope_width)...  7.13 us
    all_to_all x1, starting transfers between devices, shards(): lax.all_to_all(reply_pages, 'dp', split_axis=0, concat_axis=0, tiled=True)  6.82 us
    dynamic_slice x8, local copies, waits for them, and re-layouts, shards(): lax.map(attend, (q_nope.reshape(reqs_dev, new_len, heads_dev, nope_width)...  5.82 us
  transfers between devices with their start and end apart: 2, of which 1 were waited for; matrix products, arithmetic and copies ran while one was open for 8% of the time, Pallas kernels for 0%

commit v1 on v0

v1 whole, which is shorter than its diff:
```python
import functools
import math

import jax
import jax.numpy as jnp
from jax import lax
from jax.experimental import pallas as pl
from jax.experimental.pallas import tpu as pltpu
from jax.sharding import PartitionSpec as P

BF16 = jnp.bfloat16
F32 = jnp.float32
MASKED = -1e30
LANES = 128


def rope_rotate(rotated, position):
    half_width = rotated.shape[-1] // 2
    frequency = 10000.0 ** (-jnp.arange(half_width, dtype=F32) / half_width)
    angles = position[:, None].astype(F32) * frequency[None, :]
    cosine = jnp.cos(angles)
    sine_part = jnp.sin(angles)
    first_half = rotated[:, :half_width]
    second_half = rotated[:, half_width:]
    return jnp.concatenate(
        [
            first_half * cosine - second_half * sine_part,
            second_half * cosine + first_half * sine_part,
        ],
        axis=1,
    )


def finish_latent(raw_latent, latent_gain, position):
    width = latent_gain.shape[0]
    compressed = raw_latent[:, :width]
    mean_square = jnp.mean(compressed * compressed, axis=1, keepdims=True)
    normed = compressed * lax.rsqrt(mean_square + 1e-06) * latent_gain[None, :]
    turned = rope_rotate(raw_latent[:, width:], position)
    return jnp.concatenate([normed, turned], axis=1).astype(BF16)


def plan_body(owner_ref, slot_ref, want_ref, pick_ref):
    places = want_ref.shape[0]
    entries = pick_ref.shape[0]
    for i in range(places):
        want_ref[i] = -1
    for i in range(entries):
        first = 2 * owner_ref[i]
        place = first + jnp.where(want_ref[first] < 0, 0, 1)
        want_ref[place] = slot_ref[i]
        pick_ref[i] = place


def plan(owners, slots, places):
    smem = pl.BlockSpec(memory_space=pltpu.SMEM)
    return pl.pallas_call(
        plan_body,
        out_shape=(
            jax.ShapeDtypeStruct((places,), jnp.int32),
            jax.ShapeDtypeStruct(owners.shape, jnp.int32),
        ),
        in_specs=[smem, smem],
        out_specs=(smem, smem),
        name="plan",
    )(owners, slots)


def gather_body(ids_ref, pages_ref, out_ref):
    last = pages_ref.shape[0] - 1
    for i in range(out_ref.shape[0]):
        out_ref[i] = pages_ref[jnp.clip(ids_ref[i], 0, last)]


def gather_pages(ids, pages):
    return pl.pallas_call(
        gather_body,
        out_shape=jax.ShapeDtypeStruct((ids.shape[0],) + pages.shape[1:], pages.dtype),
        in_specs=[
            pl.BlockSpec(memory_space=pltpu.SMEM),
            pl.BlockSpec(memory_space=pltpu.VMEM),
        ],
        out_specs=pl.BlockSpec(memory_space=pltpu.VMEM),
        name="gather_pages",
    )(ids, pages)


def select_body(pick_ref, fetched_ref, out_ref, *, cols):
    entries = pick_ref.shape[0]
    per_req = entries // 2
    rows = 2 * fetched_ref.shape[1]
    width = cols * LANES
    for i in range(per_req // 2):
        tails = []
        for r in range(2):
            first = pick_ref[r * per_req + 2 * i]
            second = pick_ref[r * per_req + 2 * i + 1]
            both = jnp.concatenate(
                [fetched_ref[first].astype(F32), fetched_ref[second].astype(F32)], axis=0
            )
            at = r * LANES + i * rows
            for c in range(cols):
                out_ref[pl.ds(c * 2 * LANES + at, rows), :] = both[
                    :, c * LANES : (c + 1) * LANES
                ].astype(BF16)
            tails.append(both[:, width:])
        out_ref[pl.ds(cols * 2 * LANES + i * rows, rows), :] = jnp.concatenate(
            tails, axis=1
        ).astype(BF16)


def select_pages(pick, fetched, cols):
    return pl.pallas_call(
        functools.partial(select_body, cols=cols),
        out_shape=jax.ShapeDtypeStruct(((2 * cols + 1) * LANES, LANES), BF16),
        in_specs=[
            pl.BlockSpec(memory_space=pltpu.SMEM),
            pl.BlockSpec(memory_space=pltpu.VMEM),
        ],
        out_specs=pl.BlockSpec(memory_space=pltpu.VMEM),
        name="select_pages",
    )(pick, fetched)


def query_body(nope_ref, rope_ref, absorb_ref, out_ref):
    rows = nope_ref.shape[0]
    half = rows // 2
    nope = absorb_ref.shape[1]
    width = absorb_ref.shape[2]
    rope = rope_ref[...].astype(F32)
    turned = pltpu.roll(rope, LANES // 2, 1)
    low = lax.broadcasted_iota(jnp.int32, (half, LANES), 1) < LANES // 2
    for h in range(2):
        latent = jnp.dot(
            nope_ref[:, h * nope : (h + 1) * nope], absorb_ref[h], preferred_element_type=F32
        )
        out_ref[h, :, :width] = latent.astype(BF16)
        at_low, at_high = (rope, turned) if h == 0 else (turned, rope)
        out_ref[h, :half, width:] = jnp.where(low, at_low[:half], 0.0).astype(BF16)
        out_ref[h, half:, width:] = jnp.where(low, 0.0, at_high[half:]).astype(BF16)


def queries(q_nope, q_rope, absorb_k):
    rows = q_nope.shape[0]
    heads, nope, width = absorb_k.shape
    full = width + LANES
    return pl.pallas_call(
        query_body,
        grid=(heads // 2,),
        out_shape=jax.ShapeDtypeStruct((heads, rows, full), BF16),
        in_specs=[
            pl.BlockSpec((rows, 2 * nope), lambda i: (0, i)),
            pl.BlockSpec((rows, LANES), lambda i: (0, i)),
            pl.BlockSpec((2, nope, width), lambda i: (i, 0, 0)),
        ],
        out_specs=pl.BlockSpec((2, rows, full), lambda i: (i, 0, 0)),
        cost_estimate=pl.CostEstimate(
            flops=2 * rows * heads * nope * width,
            bytes_accessed=2 * (rows * heads * (nope + full) + heads * nope * width),
            transcendentals=0,
        ),
        name="queries",
    )(q_nope, q_rope, absorb_k)


def attend_body(*refs, pieces, has_new, first, last, factor, page, split):
    refs = list(refs)
    origin_ref = refs.pop(0)
    prefix_ref = refs.pop(0)
    query_ref = refs.pop(0)
    blocks = []
    for count in pieces:
        blocks.append([refs.pop(0) for _ in range(count)])
    if not first:
        acc_in, stat_in = refs.pop(0), refs.pop(0)
    if last:
        absorb_ref = refs.pop(0)
        out_ref = refs.pop(0)
    else:
        acc_out, stat_out = refs.pop(0), refs.pop(0)
    keys_ref, bias_ref = refs
    group, tokens, full = query_ref.shape
    width = full - LANES
    cols = width // LANES
    count = len(pieces)
    r = pl.program_id(0)

    @pl.when(pl.program_id(1) == 0)
    def _():
        for b, parts in enumerate(blocks):
            at = pl.ds(b * LANES, LANES)
            starts = []
            for part in parts:
                starts += [(part, i) for i in range(0, part.shape[0], LANES)]
            for c in range(cols):
                lows = starts[2 * c]
                keys_ref[at, c * LANES : (c + 1) * LANES] = lows[0][
                    pl.ds(lows[1] + r * LANES, LANES), :
                ]
            tail = starts[2 * cols]
            keys_ref[at, width:] = tail[0][pl.ds(tail[1], LANES), :]
            place = lax.broadcasted_iota(jnp.int32, (tokens, LANES), 1)
            if has_new and b == count - 1:
                token = lax.broadcasted_iota(jnp.int32, (tokens, LANES), 0)
                used = place <= token
            else:
                position = place // split * page + origin_ref[b] * split + place % split
                used = position < prefix_ref[r]
            bias_ref[:, b * LANES : (b + 1) * LANES] = jnp.where(used, 0.0, MASKED)

    keys = keys_ref[...]
    bias = bias_ref[...]
    for h in range(0, group, 2):
        q = query_ref[h : h + 2].reshape(2 * tokens, full)
        scores = lax.dot_general(
            q, keys, (((1,), (1,)), ((), ())), preferred_element_type=F32
        )
        scores = scores + jnp.concatenate([bias, bias], axis=0)
        top = jnp.max(scores, axis=1, keepdims=True)
        if not first:
            stat = stat_in[h : h + 2].reshape(2 * tokens, LANES)
            old_top = stat[:, 0:1]
            top = jnp.maximum(top, old_top)
        expo = jnp.exp2((scores - top) * factor)
        total = jnp.sum(expo, axis=1, keepdims=True)
        acc = jnp.dot(expo.astype(BF16), keys[:, :width], preferred_element_type=F32)
        if not first:
            alpha = jnp.exp2((old_top - top) * factor)
            total = total + alpha * stat[:, LANES // 2 : LANES // 2 + 1]
            acc = acc + alpha * acc_in[h : h + 2].reshape(2 * tokens, width).astype(F32)
        if last:
            latent = (acc / total).astype(BF16)
            for k in range(2):
                vdim = absorb_ref.shape[2]
                out_ref[:, (h + k) * vdim : (h + k + 1) * vdim] = jnp.dot(
                    latent[k * tokens : (k + 1) * tokens],
                    absorb_ref[h + k],
                    preferred_element_type=F32,
                ).astype(BF16)
        else:
            low = lax.broadcasted_iota(jnp.int32, (2 * tokens, LANES), 1) < LANES // 2
            acc_out[h : h + 2] = acc.astype(acc_out.dtype).reshape(2, tokens, width)
            stat_out[h : h + 2] = jnp.where(low, top, total).reshape(2, tokens, LANES)


def attend(query, blocks, origins, prefix_len, state, absorb_v, has_new, factor, page, split, group=4):
    heads, rows, full = query.shape
    width = full - LANES
    tokens = rows // 2
    first, last = state is None, absorb_v is not None
    smem = pl.BlockSpec(memory_space=pltpu.SMEM)
    by_head = lambda r, g: (g, r, 0)
    in_specs = [smem, smem, pl.BlockSpec((group, tokens, full), by_head)]
    args = [origins, prefix_len, query]
    for parts in blocks:
        for part in parts:
            in_specs.append(pl.BlockSpec(part.shape, lambda r, g: (0, 0)))
            args.append(part)
    acc_spec = pl.BlockSpec((group, tokens, width), by_head)
    stat_spec = pl.BlockSpec((group, tokens, LANES), by_head)
    if not first:
        in_specs += [acc_spec, stat_spec]
        args += list(state)
    if last:
        vdim = absorb_v.shape[2]
        in_specs.append(pl.BlockSpec((group, width, vdim), lambda r, g: (g, 0, 0)))
        args.append(absorb_v)
        out_shape = jax.ShapeDtypeStruct((rows, heads * vdim), BF16)
        out_specs = pl.BlockSpec((tokens, group * vdim), lambda r, g: (r, g))
    else:
        out_shape = (
            jax.ShapeDtypeStruct((heads, rows, width), BF16),
            jax.ShapeDtypeStruct((heads, rows, LANES), F32),
        )
        out_specs = (acc_spec, stat_spec)
    keys = len(blocks) * LANES
    flops = 2 * heads * rows * keys * (full + width)
    return pl.pallas_call(
        functools.partial(
            attend_body,
            pieces=tuple(len(p) for p in blocks),
            has_new=has_new,
            first=first,
            last=last,
            factor=factor,
            page=page,
            split=split,
        ),
        grid=(2, heads // group),
        out_shape=out_shape,
        in_specs=in_specs,
        out_specs=out_specs,
        scratch_shapes=[pltpu.VMEM((keys, full), BF16), pltpu.VMEM((tokens, keys), F32)],
        compiler_params=pltpu.CompilerParams(vmem_limit_bytes=48 << 20),
        cost_estimate=pl.CostEstimate(
            flops=flops,
            bytes_accessed=2 * heads * rows * (full + 2 * width),
            transcendentals=heads * rows * keys,
        ),
        name="attend",
    )(*args)


def shards(
    hidden_in,
    kv_down,
    latent_gain,
    q_nope,
    q_rope,
    absorb_k,
    absorb_v,
    store,
    page_owner,
    page_slot,
    prefix_len,
):
    rows = hidden_in.shape[0]
    reqs = prefix_len.shape[0]
    new_len = rows // reqs
    kv_rank = latent_gain.shape[0]
    lat_width = kv_down.shape[1]
    nope_width = absorb_k.shape[1]
    rope_width = lat_width - kv_rank
    page = store.shape[1]
    dp_size = lax.axis_size("dp")
    tp_size = lax.axis_size("tp")
    z = lax.axis_index("tp")
    split = page // tp_size
    cols = kv_rank // LANES

    want, pick = plan(page_owner.reshape(-1), page_slot.reshape(-1), 2 * dp_size)
    asked = lax.all_to_all(want.reshape(dp_size, 1, 2), "dp", split_axis=0, concat_axis=0, tiled=True)

    part = jnp.dot(hidden_in, kv_down, preferred_element_type=F32)
    step = tp_size // 2
    while step:
        half = part.shape[0] // 2
        upper = (z // step) % 2 == 1
        keep = jnp.where(upper, part[half:], part[:half])
        give = jnp.where(upper, part[:half], part[half:]).astype(BF16)
        got = lax.ppermute(give, "tp", [(i, i ^ step) for i in range(tp_size)])
        part = keep + got.astype(F32)
        step //= 2
    own_rows = rows // tp_size
    token = z * own_rows + jnp.arange(own_rows, dtype=jnp.int32)
    position = jnp.where(token // new_len == 0, prefix_len[0], prefix_len[1]) + token % new_len
    own_latent = finish_latent(part, latent_gain, position)
    new_latent = lax.all_gather(own_latent, "tp", axis=0, tiled=True)
    new_block = jnp.concatenate(
        [new_latent[:, c * LANES : (c + 1) * LANES] for c in range(cols)]
        + [
            jnp.concatenate(
                [new_latent[:new_len, kv_rank:], new_latent[new_len:, kv_rank:]], axis=1
            )
        ],
        axis=0,
    )

    query = queries(q_nope, q_rope, absorb_k)

    piece = lax.dynamic_slice_in_dim(store, z * split, split, axis=1)
    reply = gather_pages(asked.reshape(-1), piece)
    fetched = lax.all_to_all(
        reply.reshape(dp_size, 2, split, lat_width), "dp", split_axis=0, concat_axis=0, tiled=True
    )
    own = select_pages(pick, fetched.reshape(2 * dp_size, split, lat_width), cols)
    up = [(i, (i + 1) % tp_size) for i in range(tp_size)]
    down = [(i, (i - 1) % tp_size) for i in range(tp_size)]
    right, left = [own], [own]
    for _ in range(tp_size // 2 - 1):
        right.append(lax.ppermute(right[-1], "tp", up))
        left.append(lax.ppermute(left[-1], "tp", down))
    cut = cols * LANES
    far = [
        lax.ppermute(right[-1][:cut], "tp", up),
        lax.ppermute(left[-1][cut:], "tp", down),
    ]

    factor = math.log2(math.e) / math.sqrt(nope_width + rope_width)

    def origins(*steps):
        return jnp.stack([(z + s) % tp_size for s in steps]).astype(jnp.int32)

    common = dict(factor=factor, page=page, split=split)
    state = attend(
        query,
        [[right[1]], [left[1]], [own]],
        origins(-1, 1, 0),
        prefix_len,
        None,
        None,
        False,
        **common,
    )
    state = attend(
        query,
        [[right[2]], [left[2]], [right[3]], [left[3]]],
        origins(-2, 2, -3, 3),
        prefix_len,
        state,
        None,
        False,
        **common,
    )
    attn_out = attend(
        query,
        [far, [new_block]],
        origins(4, 0),
        prefix_len,
        state,
        absorb_v,
        True,
        **common,
    )
    return attn_out, new_latent


def solution(mesh):
    placed = (
        P("dp", "tp"),
        P("tp", None),
        P(),
        P("dp", "tp"),
        P("dp", "tp"),
        P("tp", None, None),
        P("tp", None, None),
        P("dp", None, None),
        P("dp", None, None),
        P("dp", None),
        P("dp"),
    )
    return jax.shard_map(
        shards,
        mesh=mesh,
        in_specs=placed,
        out_specs=(P("dp", "tp"), P("dp", None)),
        check_vma=False,
    )
```

time: 194 us -> 162 us (0.84)
  Pallas kernels: 0 us -> 58.2 us
  waiting for transfers between devices: 70.5 us -> 17.6 us
  starting transfers between devices: 6.86 us -> 40.2 us
  local copies, waits for them, and re-layouts: 43 us -> 10.4 us
  matrix products: 29.2 us -> 1.61 us
  blocking collectives: 12.9 us -> 27.7 us
  between operations: 14.2 us -> 0.95 us
  other arithmetic: 15.8 us -> 4.19 us
    psum x1 -> x0, waiting for transfers between devices: 70.5 us -> none  [shards(): raw_latent = lax.psum(raw_latent, 'tp')]
    pallas_call x0 -> x7, Pallas kernels: none -> 58.2 us  [the longest x3 45 us: attend(): pl.pallas_call(functools.partial(attend_body, pieces=tuple((len(p) for p...]
    all_gather x0 -> x1, blocking collectives: none -> 27.7 us  [shards(): new_latent = lax.all_gather(own_latent, 'tp', axis=0, tiled=True)]
    dot_general x7 -> x1, matrix products: 29.2 us -> 1.61 us  [shards(): part = jnp.dot(hidden_in, kv_down, preferred_element_type=F32)]
    ppermute x0 -> x11, starting transfers between devices: none -> 25.3 us  [the longest x3 12.7 us: shards(): got = lax.ppermute(give, 'tp', [(i, i ^ step) for i in range(tp_size)])]
    ppermute x0 -> x11, waiting for transfers between devices: none -> 17.6 us  [the longest x3 13.5 us: shards(): right.append(lax.ppermute(right[-1], 'tp', up))]
    all_to_all x1 -> x0, blocking collectives: 12.9 us -> none  [shards(): lax.all_to_all(want_table, 'dp', split_axis=0, concat_axis=0, tiled=True)]
    while x14 -> x0, local copies, waits for them, and re-layouts: 10.6 us -> none  [the longest x2 7.13 us: shards(): lax.map(attend, (q_nope.reshape(reqs_dev, new_len, heads_dev, nope_width)...]
  transfers between devices with their start and end apart: 2 -> 13, of which waited for: 1 -> 3; matrix products, arithmetic and copies ran while one was open for 8% -> 6% of each run, Pallas kernels for 0% -> 24%
where the time goes in v1:
time: 162 us; the launch traced here: 161 us
  Pallas kernels  58.2 us (36%)
  starting transfers between devices  40.2 us (25%)
  blocking collectives  27.7 us (17%)
  waiting for transfers between devices  17.6 us (11%)
  local copies, waits for them, and re-layouts  10.4 us (6%)
  other arithmetic  4.19 us (3%)
    pallas_call x3, Pallas kernels, attend(): pl.pallas_call(functools.partial(attend_body, pieces=tuple((len(p) for p...  45 us
    all_gather x1, blocking collectives, shards(): new_latent = lax.all_gather(own_latent, 'tp', axis=0, tiled=True)  27.7 us
    ppermute x3, waiting for transfers between devices, shards(): right.append(lax.ppermute(right[-1], 'tp', up))  13.5 us
    ppermute x3, starting transfers between devices, shards(): got = lax.ppermute(give, 'tp', [(i, i ^ step) for i in range(tp_size)])  12.7 us
    ppermute x3, starting transfers between devices, shards(): left.append(lax.ppermute(left[-1], 'tp', down))  9.84 us
    pallas_call x1, Pallas kernels, queries(): pl.pallas_call(query_body, grid=(heads // 2,), out_shape=jax.ShapeDtypeSt...  7.75 us
    all_to_all x1, starting transfers between devices, shards(): lax.all_to_all(want.reshape(dp_size, 1, 2), 'dp', split_axis=0, concat_ax...  7.61 us
    all_to_all x1, starting transfers between devices, shards(): lax.all_to_all(reply.reshape(dp_size, 2, split, lat_width), 'dp', split_a...  7.33 us
  transfers between devices with their start and end apart: 13, of which 3 were waited for; matrix products, arithmetic and copies ran while one was open for 6% of the time, Pallas kernels for 24%

profile of v1, /device:TPU:6, one launch (start us, length us, event | category | flops | bytes accessed | tf_op | source)
XLA Modules:
  0.0 160.9 jit_solution(16799176431068635500)
XLA Ops:
  1.1 1.3 reduce.6
  2.4 0.6 reshape.72.owner_ref
  3.0 1.3 reshape.73.slot_ref
  4.3 1.4 plan.1
  5.7 1.4 reshape.74
  7.1 7.6 %all-to-all-start = ((s32[32,1,2]{2,1,0:T(1,128)}), s32[32,1,2]{2,1,0:T(1,128)S(1)}, u32[]{:S(2)}, u32[]{:S(2)}) async-start(s32[32,1,2]{2,1,0:T(1,128)} %bitcast.2), calls=%async_computation | async-start | bytes 32768 | tf_op jit(solution)/shard_map/all_to_all | solution.py:332
  14.8 1.6 %fusion.12 = f32[256,576]{1,0:T(8,128)S(1)} fusion(bf16[256,896]{1,0:T(8,128)(2,1)} %param.11, bf16[896,576]{0,1:T(8,128)(2,1)S(1)} %copy-done), kind=kOutput, calls=%fused_computation.40 | convolution fusion | flops 264241152 | bytes 2080768 | tf_op jit(solution)/shard_map/dot_general | solution.py:334
  16.4 7.3 %collective-permute-start.8 = (bf16[128,576]{1,0:T(8,128)(2,1)S(1)}, bf16[128,576]{1,0:T(8,128)(2,1)S(1)}, u32[]{:S(2)}, u32[]{:S(2)}) collective-permute-start(bf16[128,576]{1,0:T(8,128)(2,1)S(1)} %select_convert_fusion), channel_id=1, source_target_pairs={{0,4},{1,5},{2,6},{3,7},{4,0},{5,1},{6,2},{7,3},{8,12},{9,13},{10,... | collective-permute-start | bytes 442376 | tf_op jit(solution)/shard_map/ppermute | solution.py:341
  23.7 1.4 fusion.11
  25.3 1.4 fusion.9
  26.7 1.9 %constant_dynamic-slice_fusion.pages_ref = bf16[48,8,576]{2,1,0:T(8,128)(2,1)} fusion(bf16[48,64,576]{2,1,0:T(8,128)(2,1)} %param.18, s32[]{:T(128)S(6)} %select_n.125), kind=kLoop, calls=%fused_computation.37 | loop fusion | bytes 884740 | tf_op jit(solution)/shard_map/dynamic_slice | solution.py:361
  28.7 5.1 %collective-permute-start.9 = (bf16[64,576]{1,0:T(8,128)(2,1)S(1)}, bf16[64,576]{1,0:T(8,128)(2,1)S(1)}, u32[]{:S(2)}, u32[]{:S(2)}) collective-permute-start(bf16[64,576]{1,0:T(8,128)(2,1)S(1)} %select_convert_fusion.1), channel_id=1, source_target_pairs={{0,2},{1,3},{2,0},{3,1},{4,6},{5,7},{6,4},{7,5},{8,10},{9,11},{10,... | collective-permute-start | bytes 221192 | tf_op jit(solution)/shard_map/ppermute | solution.py:341
  33.9 4.1 %collective-permute-done.9 = bf16[64,576]{1,0:T(8,128)(2,1)S(1)} collective-permute-done((bf16[64,576]{1,0:T(8,128)(2,1)S(1)}, bf16[64,576]{1,0:T(8,128)(2,1)S(1)}, u32[]{:S(2)}, u32[]{:S(2)}) %collective-permute-start.9) | collective-permute-done | bytes 73760 | tf_op jit(solution)/shard_map/ppermute | solution.py:341
  38.3 7.8 %queries.1.refs_2_ = bf16[16,256,640]{2,1,0:T(8,128)(2,1)} custom-call(bf16[256,2048]{1,0:T(8,128)(2,1)} %nope_ref.1, bf16[256,1024]{1,0:T(8,128)(2,1)} %rope_ref.1, bf16[16,128,512]{2,1,0:T(8,128)(2,1)} %absorb_ref.1), custom_call_target="tpu_custom_call" | custom-call | flops 536870912 | bytes 8388608 | tf_op jit(solution)/shard_map/queries/pallas_call | solution.py:147
  46.1 0.6 reduce.7
  46.7 0.6 reshape.75.ids_ref
  47.3 2.0 %gather_pages.1 = bf16[64,8,576]{2,1,0:T(8,128)(2,1)} custom-call(s32[64]{0:T(128)} %reshape.75.ids_ref, bf16[48,8,576]{2,1,0:T(8,128)(2,1)} %constant_dynamic-slice_fusion.pages_ref), custom_call_target="tpu_custom_call" | custom-call | tf_op jit(solution)/shard_map/gather_pages/pallas_call | solution.py:76
  49.3 7.3 %all-to-all-start.1 = ((bf16[32,2,8,576]{3,2,1,0:T(8,128)(2,1)}), bf16[32,2,8,576]{3,2,1,0:T(8,128)(2,1)S(1)}, u32[]{:S(2)}, u32[]{:S(2)}) async-start(bf16[32,2,8,576]{3,2,1,0:T(8,128)(2,1)} %bitcast.17), calls=%async_computation.1 | async-start | bytes 1310720 | tf_op jit(solution)/shard_map/all_to_all | solution.py:363
  57.1 27.7 %all_gather.3 = bf16[256,576]{1,0:T(8,128)(2,1)S(1)} all-gather(bf16[32,576]{1,0:T(8,128)(2,1)S(1)} %pad_maximum_fusion), channel_id=1, replica_groups=mesh['dp'=32,'tp'=8] {'tp'}, dimensions={0}, use_global_device_ids=true | all-gather | bytes 331776 | tf_op jit(solution)/shard_map/all_gather | solution.py:348
  84.9 0.8 copy-done.4
  85.8 1.9 %select_pages.1.refs_5_ = bf16[1152,128]{1,0:T(8,128)(2,1)} custom-call(s32[32]{0:T(128)} %get-tuple-element.8.pick_ref, bf16[64,8,576]{2,1,0:T(8,128)(2,1)} %bitcast.16), custom_call_target="tpu_custom_call" | custom-call | tf_op jit(solution)/shard_map/select_pages/pallas_call | solution.py:113
  88.1 2.8 %collective-permute-start.4 = (bf16[1152,128]{1,0:T(8,128)(2,1)}, bf16[1152,128]{1,0:T(8,128)(2,1)S(1)}, u32[]{:S(2)}, u32[]{:S(2)}) collective-permute-start(bf16[1152,128]{1,0:T(8,128)(2,1)} %select_pages.1.refs_5_), channel_id=1, source_target_pairs={{0,7},{1,0},{2,1},{3,2},{4,3},{5,4},{6,5},{7,6},{8,15},{9,8},{10,9... | collective-permute-start | bytes 884744 | tf_op jit(solution)/shard_map/ppermute | solution.py:372
  90.9 0.9 copy.22
  91.8 6.9 %collective-permute-done.refs_3_ = bf16[1152,128]{1,0:T(8,128)(2,1)S(1)} collective-permute-done((bf16[1152,128]{1,0:T(8,128)(2,1)}, bf16[1152,128]{1,0:T(8,128)(2,1)S(1)}, u32[]{:S(2)}, u32[]{:S(2)}) %collective-permute-start) | collective-permute-done | bytes 294944 | tf_op jit(solution)/shard_map/ppermute | solution.py:371
  98.7 3.5 %collective-permute-start.5 = (bf16[1152,128]{1,0:T(8,128)(2,1)S(1)}, bf16[1152,128]{1,0:T(8,128)(2,1)S(1)}, u32[]{:S(2)}, u32[]{:S(2)}) collective-permute-start(bf16[1152,128]{1,0:T(8,128)(2,1)S(1)} %collective-permute-done.4.refs_4_), channel_id=1, source_target_pairs={{0,7},{1,0},{2,1},{3,2},{4,3},{5,4},{6,5},{7,6},{8,15},{9,8},{10,9... | collective-permute-start | bytes 884744 | tf_op jit(solution)/shard_map/ppermute | solution.py:372
  102.3 6.6 %collective-permute-done.1.refs_3_ = bf16[1152,128]{1,0:T(8,128)(2,1)S(1)} collective-permute-done((bf16[1152,128]{1,0:T(8,128)(2,1)S(1)}, bf16[1152,128]{1,0:T(8,128)(2,1)S(1)}, u32[]{:S(2)}, u32[]{:S(2)}) %collective-permute-start.1) | collective-permute-done | bytes 294944 | tf_op jit(solution)/shard_map/ppermute | solution.py:371
  109.0 3.5 %collective-permute-start.6 = (bf16[1152,128]{1,0:T(8,128)(2,1)S(1)}, bf16[1152,128]{1,0:T(8,128)(2,1)S(1)}, u32[]{:S(2)}, u32[]{:S(2)}) collective-permute-start(bf16[1152,128]{1,0:T(8,128)(2,1)S(1)} %collective-permute-done.5.refs_4_), channel_id=1, source_target_pairs={{0,7},{1,0},{2,1},{3,2},{4,3},{5,4},{6,5},{7,6},{8,15},{9,8},{10,9... | collective-permute-start | bytes 884744 | tf_op jit(solution)/shard_map/ppermute | solution.py:372
  112.5 1.0 copy-done.2
  113.4 12.4 %attend.3 = (bf16[16,256,512]{2,1,0:T(8,128)(2,1)}, f32[16,256,128]{2,1,0:T(8,128)S(1)}) custom-call(s32[3]{0:T(128)S(1)} %pad_add_fusion.2.refs_0_, s32[2]{0:T(128)S(1)} %copy-done.3, bf16[16,256,640]{2,1,0:T(8,128)(2,1)} %queries.1.refs_2_, bf16[1152,128]{1,0:T(8,128)(2,1)S(1)} %collective-permute-done.refs_3_, ...), custom_call_target="tpu_custom_call" | custom-call | flops 3623878656 | bytes 13631488 | tf_op jit(solution)/shard_map/attend/pallas_call | solution.py:278
  126.0 2.3 %collective-permute-start.3 = (bf16[512,128]{1,0:T(8,128)(2,1)S(1)}, bf16[512,128]{1,0:T(8,128)(2,1)S(1)}, u32[]{:S(2)}, u32[]{:S(2)}) collective-permute-start(bf16[512,128]{1,0:T(8,128)(2,1)S(1)} %slice.85), channel_id=1, source_target_pairs={{0,1},{1,2},{2,3},{3,4},{4,5},{5,6},{6,7},{7,0},{8,9},{9,10},{10,1... | collective-permute-start | bytes 393224 | tf_op jit(solution)/shard_map/ppermute | solution.py:375
  128.2 15.8 %attend.4 = (bf16[16,256,512]{2,1,0:T(8,128)(2,1)}, f32[16,256,128]{2,1,0:T(8,128)S(1)}) custom-call(s32[4]{0:T(128)S(1)} %pad_add_fusion.1.refs_0_, s32[2]{0:T(128)S(1)} %copy-done.3, bf16[16,256,640]{2,1,0:T(8,128)(2,1)} %queries.1.refs_2_, bf16[1152,128]{1,0:T(8,128)(2,1)S(1)} %collective-permute-done.1.refs_3_, ...), custom_call_target="tpu_custom_call" | custom-call | flops 4831838208 | bytes 13631488 | tf_op jit(solution)/shard_map/attend/pallas_call | solution.py:278
  144.0 16.9 %attend.5 = bf16[256,2048]{1,0:T(8,128)(2,1)} custom-call(s32[2]{0:T(128)S(1)} %pad_add_fusion.refs_0_, s32[2]{0:T(128)S(1)} %copy-done.3, bf16[16,256,640]{2,1,0:T(8,128)(2,1)} %queries.1.refs_2_, bf16[512,128]{1,0:T(8,128)(2,1)S(1)} %collective-permute-done.3.refs_3_, bf16[640,128]{1,0:T(8,128)(2,1)S(1)} %collective-permute-done.7.refs_4_, ...), custom_call_target="tpu_custom_call" | custom-call | flops 2415919104 | bytes 13631488 | tf_op jit(solution)/shard_map/attend/pallas_call | solution.py:278
  (49 shorter events, 2.4 us)
Async XLA Ops:
  0.6 14.1 %copy-start = (bf16[896,576]{0,1:T(8,128)(2,1)S(1)}, bf16[896,576]{0,1:T(8,128)(2,1)}, u32[]{:S(2)}) copy-start(bf16[896,576]{0,1:T(8,128)(2,1)} %param.12) | copy-start | bytes 3096580
  7.1 39.0 %all-to-all-start = ((s32[32,1,2]{2,1,0:T(1,128)}), s32[32,1,2]{2,1,0:T(1,128)S(1)}, u32[]{:S(2)}, u32[]{:S(2)}) async-start(s32[32,1,2]{2,1,0:T(1,128)} %bitcast.2), calls=%async_computation | async-start | bytes 32768 | tf_op jit(solution)/shard_map/all_to_all | solution.py:332
  16.4 12.2 %collective-permute-start.8 = (bf16[128,576]{1,0:T(8,128)(2,1)S(1)}, bf16[128,576]{1,0:T(8,128)(2,1)S(1)}, u32[]{:S(2)}, u32[]{:S(2)}) collective-permute-start(bf16[128,576]{1,0:T(8,128)(2,1)S(1)} %select_convert_fusion), channel_id=1, source_target_pairs={{0,4},{1,5},{2,6},{3,7},{4,0},{5,1},{6,2},{7,3},{8,12},{9,13},{10,... | collective-permute-start | bytes 442376 | tf_op jit(solution)/shard_map/ppermute | solution.py:341
  28.7 9.2 %collective-permute-start.9 = (bf16[64,576]{1,0:T(8,128)(2,1)S(1)}, bf16[64,576]{1,0:T(8,128)(2,1)S(1)}, u32[]{:S(2)}, u32[]{:S(2)}) collective-permute-start(bf16[64,576]{1,0:T(8,128)(2,1)S(1)} %select_convert_fusion.1), channel_id=1, source_target_pairs={{0,2},{1,3},{2,0},{3,1},{4,6},{5,7},{6,4},{7,5},{8,10},{9,11},{10,... | collective-permute-start | bytes 221192 | tf_op jit(solution)/shard_map/ppermute | solution.py:341
  38.0 18.9 %copy-start.5 = (f32[512]{0:T(512)S(1)}, f32[512]{0:T(512)}, u32[]{:S(2)}) copy-start(f32[512]{0:T(512)} %param.13) | copy-start | bytes 6148
  38.0 18.7 %collective-permute-start.10 = (bf16[32,576]{1,0:T(8,128)(2,1)S(1)}, bf16[32,576]{1,0:T(8,128)(2,1)S(1)}, u32[]{:S(2)}, u32[]{:S(2)}) collective-permute-start(bf16[32,576]{1,0:T(8,128)(2,1)S(1)} %select_convert_fusion.2), channel_id=1, source_target_pairs={{0,1},{1,0},{2,3},{3,2},{4,5},{5,4},{6,7},{7,6},{8,9},{9,8},{10,11... | collective-permute-start | bytes 110600 | tf_op jit(solution)/shard_map/ppermute | solution.py:341
  46.1 66.4 %copy-start.3 = (s32[2]{0:T(128)S(1)}, s32[2]{0:T(128)}, u32[]{:S(2)}) copy-start(s32[2]{0:T(128)} %refs_1_.5) | copy-start | bytes 28
  49.3 35.6 %all-to-all-start.1 = ((bf16[32,2,8,576]{3,2,1,0:T(8,128)(2,1)}), bf16[32,2,8,576]{3,2,1,0:T(8,128)(2,1)S(1)}, u32[]{:S(2)}, u32[]{:S(2)}) async-start(bf16[32,2,8,576]{3,2,1,0:T(8,128)(2,1)} %bitcast.17), calls=%async_computation.1 | async-start | bytes 1310720 | tf_op jit(solution)/shard_map/all_to_all | solution.py:363
  84.9 0.8 copy-start.4
  87.7 11.0 %collective-permute-start = (bf16[1152,128]{1,0:T(8,128)(2,1)}, bf16[1152,128]{1,0:T(8,128)(2,1)S(1)}, u32[]{:S(2)}, u32[]{:S(2)}) collective-permute-start(bf16[1152,128]{1,0:T(8,128)(2,1)} %select_pages.1.refs_5_), channel_id=1, source_target_pairs={{0,1},{1,2},{2,3},{3,4},{4,5},{5,6},{6,7},{7,0},{8,9},{9,10},{10,1... | collective-permute-start | bytes 884744 | tf_op jit(solution)/shard_map/ppermute | solution.py:371
  88.1 10.6 %collective-permute-start.4 = (bf16[1152,128]{1,0:T(8,128)(2,1)}, bf16[1152,128]{1,0:T(8,128)(2,1)S(1)}, u32[]{:S(2)}, u32[]{:S(2)}) collective-permute-start(bf16[1152,128]{1,0:T(8,128)(2,1)} %select_pages.1.refs_5_), channel_id=1, source_target_pairs={{0,7},{1,0},{2,1},{3,2},{4,3},{5,4},{6,5},{7,6},{8,15},{9,8},{10,9... | collective-permute-start | bytes 884744 | tf_op jit(solution)/shard_map/ppermute | solution.py:372
  98.7 10.2 %collective-permute-start.1 = (bf16[1152,128]{1,0:T(8,128)(2,1)S(1)}, bf16[1152,128]{1,0:T(8,128)(2,1)S(1)}, u32[]{:S(2)}, u32[]{:S(2)}) collective-permute-start(bf16[1152,128]{1,0:T(8,128)(2,1)S(1)} %collective-permute-done.refs_3_), channel_id=1, source_target_pairs={{0,1},{1,2},{2,3},{3,4},{4,5},{5,6},{6,7},{7,0},{8,9},{9,10},{10,1... | collective-permute-start | bytes 884744 | tf_op jit(solution)/shard_map/ppermute | solution.py:371
  98.7 10.2 %collective-permute-start.5 = (bf16[1152,128]{1,0:T(8,128)(2,1)S(1)}, bf16[1152,128]{1,0:T(8,128)(2,1)S(1)}, u32[]{:S(2)}, u32[]{:S(2)}) collective-permute-start(bf16[1152,128]{1,0:T(8,128)(2,1)S(1)} %collective-permute-done.4.refs_4_), channel_id=1, source_target_pairs={{0,7},{1,0},{2,1},{3,2},{4,3},{5,4},{6,5},{7,6},{8,15},{9,8},{10,9... | collective-permute-start | bytes 884744 | tf_op jit(solution)/shard_map/ppermute | solution.py:372
  108.9 17.0 %collective-permute-start.2 = (bf16[1152,128]{1,0:T(8,128)(2,1)S(1)}, bf16[1152,128]{1,0:T(8,128)(2,1)S(1)}, u32[]{:S(2)}, u32[]{:S(2)}) collective-permute-start(bf16[1152,128]{1,0:T(8,128)(2,1)S(1)} %collective-permute-done.1.refs_3_), channel_id=1, source_target_pairs={{0,1},{1,2},{2,3},{3,4},{4,5},{5,6},{6,7},{7,0},{8,9},{9,10},{10,1... | collective-permute-start | bytes 884744 | tf_op jit(solution)/shard_map/ppermute | solution.py:371
  109.0 16.9 %collective-permute-start.6 = (bf16[1152,128]{1,0:T(8,128)(2,1)S(1)}, bf16[1152,128]{1,0:T(8,128)(2,1)S(1)}, u32[]{:S(2)}, u32[]{:S(2)}) collective-permute-start(bf16[1152,128]{1,0:T(8,128)(2,1)S(1)} %collective-permute-done.5.refs_4_), channel_id=1, source_target_pairs={{0,7},{1,0},{2,1},{3,2},{4,3},{5,4},{6,5},{7,6},{8,15},{9,8},{10,9... | collective-permute-start | bytes 884744 | tf_op jit(solution)/shard_map/ppermute | solution.py:372
  112.5 1.0 copy-start.2
  125.8 18.2 %collective-permute-start.7 = (bf16[640,128]{1,0:T(8,128)(2,1)S(1)}, bf16[640,128]{1,0:T(8,128)(2,1)S(1)}, u32[]{:S(2)}, u32[]{:S(2)}) collective-permute-start(bf16[640,128]{1,0:T(8,128)(2,1)S(1)} %slice.86), channel_id=1, source_target_pairs={{0,7},{1,0},{2,1},{3,2},{4,3},{5,4},{6,5},{7,6},{8,15},{9,8},{10,9... | collective-permute-start | bytes 491528 | tf_op jit(solution)/shard_map/ppermute | solution.py:376
  126.0 18.0 %collective-permute-start.3 = (bf16[512,128]{1,0:T(8,128)(2,1)S(1)}, bf16[512,128]{1,0:T(8,128)(2,1)S(1)}, u32[]{:S(2)}, u32[]{:S(2)}) collective-permute-start(bf16[512,128]{1,0:T(8,128)(2,1)S(1)} %slice.85), channel_id=1, source_target_pairs={{0,1},{1,2},{2,3},{3,4},{4,5},{5,6},{6,7},{7,0},{8,9},{9,10},{10,1... | collective-permute-start | bytes 393224 | tf_op jit(solution)/shard_map/ppermute | solution.py:375
  128.2 15.8 %copy-start.1 = (bf16[16,512,128]{2,1,0:T(8,128)(2,1)S(1)}, bf16[16,512,128]{2,1,0:T(8,128)(2,1)}, u32[]{:S(2)}) copy-start(bf16[16,512,128]{2,1,0:T(8,128)(2,1)} %refs_8_.1) | copy-start | bytes 6291460

commit v2 on v0

v2 whole, which is shorter than its diff:
```python
import functools
import math

import jax
import jax.numpy as jnp
from jax import lax
from jax.experimental import pallas as pl
from jax.experimental.pallas import tpu as pltpu
from jax.sharding import PartitionSpec as P

BF16 = jnp.bfloat16
F32 = jnp.float32
MASKED = -1e30
LANES = 128


def turn_tables(position, half_width):
    frequency = 10000.0 ** (-jnp.arange(half_width, dtype=F32) / half_width)
    angles = position[:, None].astype(F32) * frequency[None, :]
    return jnp.cos(angles), jnp.sin(angles)


VMEM = pl.BlockSpec(memory_space=pltpu.VMEM)
SMEM = pl.BlockSpec(memory_space=pltpu.SMEM)
SMALL = pltpu.CompilerParams(vmem_limit_bytes=4 << 20)


def deal_body(place_ref, hidden_ref, down_ref, keep_ref, *rest):
    part_ref = rest[-1]
    part_ref[...] = lax.dot_general(
        hidden_ref[...], down_ref[...], (((1,), (1,)), ((), ())), preferred_element_type=F32
    )
    rows = keep_ref.shape[0]
    keep_ref[...] = part_ref[pl.ds(pl.multiple_of(place_ref[0] * rows, rows), rows), :]
    for i, give_ref in enumerate(rest[:-1]):
        other = pl.multiple_of(place_ref[1 + i] * rows, rows)
        give_ref[...] = part_ref[pl.ds(other, rows), :].astype(BF16)


def deal(place, hidden, down, members):
    rows, width = hidden.shape[0] // members, down.shape[0]
    return pl.pallas_call(
        deal_body,
        out_shape=(jax.ShapeDtypeStruct((rows, width), F32),)
        + (jax.ShapeDtypeStruct((rows, width), BF16),) * (members - 1),
        in_specs=[SMEM, VMEM, VMEM],
        out_specs=(VMEM,) * members,
        scratch_shapes=[pltpu.VMEM((hidden.shape[0], width), F32)],
        compiler_params=SMALL,
        name="deal",
    )(place, hidden, down)


def finish_body(kept_ref, gain_ref, cos_ref, sin_ref, *rest):
    out_ref = rest[-1]
    width = gain_ref.shape[1]
    raw = kept_ref[...]
    for got_ref in rest[:-1]:
        raw = raw + got_ref[...].astype(F32)
    compressed = raw[:, :width]
    mean_square = jnp.mean(compressed * compressed, axis=1, keepdims=True)
    latent = (compressed * lax.rsqrt(mean_square + 1e-06) * gain_ref[...]).astype(BF16)
    half = cos_ref.shape[1]
    first, second = raw[:, width : width + half], raw[:, width + half :]
    cosine, sine = cos_ref[...], sin_ref[...]
    turned = jnp.concatenate(
        [first * cosine - second * sine, second * cosine + first * sine], axis=1
    )
    rows = raw.shape[0]
    for c in range(width // LANES):
        out_ref[c * rows : (c + 1) * rows, :] = latent[:, c * LANES : (c + 1) * LANES]
    out_ref[width // LANES * rows :, :] = jnp.concatenate(
        [turned[: rows // 2], turned[rows // 2 :]], axis=1
    ).astype(BF16)


def finish_latents(kept, gain, cosine, sine, got):
    rows, width = kept.shape[0], gain.shape[1]
    return pl.pallas_call(
        finish_body,
        out_shape=jax.ShapeDtypeStruct((width // LANES * rows + rows // 2, LANES), BF16),
        in_specs=[VMEM] * (4 + len(got)),
        out_specs=VMEM,
        compiler_params=SMALL,
        name="finish_latents",
    )(kept, gain, cosine, sine, *got)


def plan_body(owner_ref, slot_ref, want_ref, pick_ref):
    reqs, pages = owner_ref.shape
    for owner in range(want_ref.shape[0]):
        want_ref[owner, 0, 0] = -1
        want_ref[owner, 0, 1] = -1
    for r in range(reqs):
        for i in range(pages):
            owner = owner_ref[r, i]
            rank = jnp.where(want_ref[owner, 0, 0] < 0, 0, 1)
            want_ref[owner, 0, rank] = slot_ref[r, i]
            pick_ref[r * pages + i] = 2 * owner + rank


def plan(owners, slots, dp_size):
    smem = pl.BlockSpec(memory_space=pltpu.SMEM)
    return pl.pallas_call(
        plan_body,
        out_shape=(
            jax.ShapeDtypeStruct((dp_size, 1, 2), jnp.int32),
            jax.ShapeDtypeStruct((owners.size,), jnp.int32),
        ),
        in_specs=[smem, smem],
        out_specs=(smem, smem),
        name="plan",
    )(owners, slots)


def gather_body(ids_ref, pages_ref, out_ref):
    last = pages_ref.shape[0] - 1
    for i in range(ids_ref.shape[0]):
        for j in range(2):
            out_ref[i, j] = pages_ref[jnp.clip(ids_ref[i, 0, j], 0, last)]


def gather_pages(ids, pages):
    return pl.pallas_call(
        gather_body,
        out_shape=jax.ShapeDtypeStruct((ids.shape[0], 2) + pages.shape[1:], pages.dtype),
        in_specs=[
            pl.BlockSpec(memory_space=pltpu.SMEM),
            pl.BlockSpec(memory_space=pltpu.VMEM),
        ],
        out_specs=pl.BlockSpec(memory_space=pltpu.VMEM),
        compiler_params=pltpu.CompilerParams(vmem_limit_bytes=4 << 20),
        name="gather_pages",
    )(ids, pages)


def select_body(pick_ref, fetched_ref, fresh_ref, out_ref, *, cols):
    out_ref[(2 * cols + 1) * LANES :, :] = fresh_ref[...]
    entries = pick_ref.shape[0]
    per_req = entries // 2
    rows = 2 * fetched_ref.shape[1]
    width = cols * LANES
    for i in range(per_req // 2):
        tails = []
        for r in range(2):
            first = pick_ref[r * per_req + 2 * i]
            second = pick_ref[r * per_req + 2 * i + 1]
            both = jnp.concatenate(
                [fetched_ref[first].astype(F32), fetched_ref[second].astype(F32)], axis=0
            )
            at = r * LANES + i * rows
            for c in range(cols):
                out_ref[pl.ds(c * 2 * LANES + at, rows), :] = both[
                    :, c * LANES : (c + 1) * LANES
                ].astype(BF16)
            tails.append(both[:, width:])
        out_ref[pl.ds(cols * 2 * LANES + i * rows, rows), :] = jnp.concatenate(
            tails, axis=1
        ).astype(BF16)


def select_pages(pick, fetched, fresh, cols):
    return pl.pallas_call(
        functools.partial(select_body, cols=cols),
        out_shape=jax.ShapeDtypeStruct(((2 * cols + 1) * LANES + fresh.shape[0], LANES), BF16),
        in_specs=[
            SMEM,
            VMEM,
            VMEM,
        ],
        out_specs=VMEM,
        compiler_params=SMALL,
        name="select_pages",
    )(pick, fetched, fresh)


def query_body(nope_ref, rope_ref, absorb_ref, out_ref):
    rows = nope_ref.shape[0]
    half = rows // 2
    heads, nope, width = absorb_ref.shape
    side = LANES // 2
    for p in range(heads // 2):
        rope = rope_ref[:, p * LANES : (p + 1) * LANES].T
        for h in range(2):
            n = 2 * p + h
            latent = lax.dot_general(
                absorb_ref[n],
                nope_ref[:, n * nope : (n + 1) * nope],
                (((0,), (1,)), ((), ())),
                preferred_element_type=F32,
            ).astype(BF16)
            at = slice(h * LANES, (h + 1) * LANES)
            for r in range(2):
                out_ref[p, r, :width, at] = latent[:, r * half : (r + 1) * half]
                put, skip = width + r * side, width + (1 - r) * side
                out_ref[p, r, put : put + side, at] = rope[
                    h * side : (h + 1) * side, r * half : (r + 1) * half
                ]
                out_ref[p, r, skip : skip + side, at] = jnp.zeros((side, LANES), BF16)


def queries(q_nope, q_rope, absorb_k):
    rows = q_nope.shape[0]
    heads, _, width = absorb_k.shape
    vmem = pl.BlockSpec(memory_space=pltpu.VMEM)
    return pl.pallas_call(
        query_body,
        out_shape=jax.ShapeDtypeStruct((heads // 2, 2, width + LANES, rows), BF16),
        in_specs=[vmem] * 3,
        out_specs=vmem,
        compiler_params=pltpu.CompilerParams(vmem_limit_bytes=16 << 20),
        name="queries",
    )(q_nope, q_rope, absorb_k)


def lay_block(parts, b, r, step, origin_ref, prefix_ref, keys_ref, values_ref, bias_ref, page, split):
    width = values_ref.shape[0]
    at = slice(b * LANES, (b + 1) * LANES)
    starts = []
    for part in parts:
        starts += [(part, i) for i in range(0, part.shape[0], LANES)]
    for c in range(width // LANES):
        ref, low = starts[2 * c + r]
        tile = ref[low : low + LANES, :]
        keys_ref[at, c * LANES : (c + 1) * LANES] = tile
        values_ref[c * LANES : (c + 1) * LANES, at] = tile.T
    ref, low = starts[2 * (width // LANES)]
    keys_ref[at, width:] = ref[low : low + LANES, :]
    place = lax.broadcasted_iota(jnp.int32, (LANES, LANES), 0)
    position = place // split * page + origin_ref[step] * split + place % split
    bias_ref[at, :] = jnp.where(position < prefix_ref[r], 0.0, MASKED)


def join_new(tails, origin_ref, new_ref):
    for ref, low, step in tails:
        rows = (ref.shape[0] - low) * 2 // 9
        first = pl.multiple_of(origin_ref[step] * rows, rows)
        for c in range(4):
            new_ref[pl.ds(first, rows), c * LANES : (c + 1) * LANES] = ref[
                low + c * rows : low + (c + 1) * rows, :
            ]
        turned = ref[low + 4 * rows :, :]
        half = rows // 2
        for h in range(2):
            place = pl.multiple_of(first + h * half, half)
            new_ref[pl.ds(place, half), 4 * LANES :] = turned[
                :, h * LANES // 2 : (h + 1) * LANES // 2
            ]


def lay_new(new_ref, b, r, keys_ref, values_ref, bias_ref):
    width = values_ref.shape[0]
    side = LANES // 2
    at = slice(b * LANES, (b + 1) * LANES)
    rows = slice(r * LANES, (r + 1) * LANES)
    for c in range(width // LANES):
        tile = new_ref[rows, c * LANES : (c + 1) * LANES]
        keys_ref[at, c * LANES : (c + 1) * LANES] = tile
        values_ref[c * LANES : (c + 1) * LANES, at] = tile.T
    put, skip = width + r * side, width + (1 - r) * side
    keys_ref[at, put : put + side] = new_ref[rows, width:]
    keys_ref[at, skip : skip + side] = jnp.zeros((LANES, side), BF16)
    place = lax.broadcasted_iota(jnp.int32, (LANES, LANES), 0)
    token = lax.broadcasted_iota(jnp.int32, (LANES, LANES), 1)
    bias_ref[at, :] = jnp.where(place <= token, 0.0, MASKED)


def attend_body(*refs, pieces, steps, seen_steps, full_width, first, last, factor, page, split):
    refs = list(refs)
    origin_ref, prefix_ref, query_ref = [refs.pop(0) for _ in range(3)]
    blocks = [[refs.pop(0) for _ in range(n)] for n in pieces]
    if not first:
        acc_in, stat_in = refs.pop(0), refs.pop(0)
    if last:
        seen = [refs.pop(0) for _ in seen_steps]
        absorb_ref, out_ref, turned_ref, new_ref = [refs.pop(0) for _ in range(3)] + [refs.pop()]
        low = (full_width // LANES * 2 - 1) * LANES
        tails = [(ref, low, step) for ref, step in zip(seen, seen_steps)]
        cut = blocks[0][0].shape[0]
        join_new(tails + [(blocks[0][1], low - cut, steps[0])], origin_ref, new_ref)
    else:
        acc_out, stat_out = refs.pop(0), refs.pop(0)
    keys_ref, values_ref, bias_ref = refs
    pairs, reqs, full, lanes = query_ref.shape

    def score(r, k):
        s = jnp.dot(keys_ref[r], query_ref[k, r], preferred_element_type=F32)
        bias = bias_ref[r]
        return s + jnp.concatenate([bias, bias], axis=1)

    def finish(r, k, s):
        top = jnp.max(s, axis=0, keepdims=True)
        if not first:
            old_top = stat_in[k, r, 0:1, :]
            top = jnp.maximum(top, old_top)
        expo = jnp.exp2((s - top) * factor)
        total = jnp.sum(expo, axis=0, keepdims=True)
        acc = jnp.dot(values_ref[r], expo.astype(BF16), preferred_element_type=F32)
        if not first:
            alpha = jnp.exp2((old_top - top) * factor)
            total = total + alpha * stat_in[k, r, 1:2, :]
            acc = acc + alpha * acc_in[k, r].astype(F32)
        if last:
            latent = (acc * (1.0 / total)).astype(BF16)
            vdim = absorb_ref.shape[2]
            tokens = lanes // 2
            for h in range(2):
                n = 2 * k + h
                out_ref[r * tokens : (r + 1) * tokens, n * vdim : (n + 1) * vdim] = lax.dot_general(
                    latent[:, h * tokens : (h + 1) * tokens],
                    absorb_ref[n],
                    (((0,), (0,)), ((), ())),
                    preferred_element_type=F32,
                ).astype(BF16)
        else:
            acc_out[k, r] = acc.astype(BF16)
            stat_out[k, r, 0:1, :] = top
            stat_out[k, r, 1:2, :] = total

    for r in range(reqs):
        for b, parts in enumerate(blocks):
            lay_block(
                parts, b, r, steps[b], origin_ref, prefix_ref,
                keys_ref.at[r], values_ref.at[r], bias_ref.at[r], page, split,
            )
        if last:
            lay_new(new_ref, len(blocks), r, keys_ref.at[r], values_ref.at[r], bias_ref.at[r])
            own = slice(r * LANES, (r + 1) * LANES)
            turned_ref[: full - LANES, own] = values_ref[r, :, len(blocks) * LANES :]
            turned_ref[full - LANES :, own] = new_ref[own, full - LANES :].T
    order = [(r, k) for r in range(reqs) for k in range(pairs)]
    s = score(*order[0])
    for i, (r, k) in enumerate(order):
        following = score(*order[i + 1]) if i + 1 < len(order) else None
        finish(r, k, s)
        s = following


def attend(
    query, blocks, steps, origins, prefix_len, factor, page, split, state=None, absorb_v=None, seen=()
):
    pairs, reqs, full, lanes = query.shape
    width = full - LANES
    first, last = state is None, absorb_v is not None
    args = [query] + [part for parts in blocks for part in parts]
    aliases = {}
    if not first:
        if not last:
            aliases = {2 + len(args): 0, 3 + len(args): 1}
        args += list(state)
    if last:
        args += [block for _, block in seen] + [absorb_v]
        vdim = absorb_v.shape[2]
        out_shape = (
            jax.ShapeDtypeStruct((reqs * lanes // 2, 2 * pairs * vdim), BF16),
            jax.ShapeDtypeStruct((width + LANES // 2, reqs * lanes // 2), BF16),
        )
    else:
        out_shape = (
            jax.ShapeDtypeStruct((pairs, reqs, width, lanes), BF16),
            jax.ShapeDtypeStruct((pairs, reqs, 8, lanes), F32),
        )
    keys = (len(blocks) + last) * LANES
    return pl.pallas_call(
        functools.partial(
            attend_body,
            pieces=tuple(len(parts) for parts in blocks),
            steps=steps,
            seen_steps=tuple(step for step, _ in seen),
            full_width=full,
            first=first,
            last=last,
            factor=factor,
            page=page,
            split=split,
        ),
        out_shape=out_shape,
        in_specs=[SMEM, SMEM] + [VMEM] * len(args),
        out_specs=(VMEM, VMEM),
        input_output_aliases=aliases,
        scratch_shapes=[
            pltpu.VMEM((reqs, keys, full), BF16),
            pltpu.VMEM((reqs, width, keys), BF16),
            pltpu.VMEM((reqs, keys, LANES), F32),
        ]
        + [pltpu.VMEM((reqs * lanes // 2, width + LANES // 2), BF16)] * last,
        compiler_params=pltpu.CompilerParams(vmem_limit_bytes=16 << 20),
        cost_estimate=pl.CostEstimate(
            flops=2 * pairs * reqs * lanes * keys * (full + width),
            bytes_accessed=2 * pairs * reqs * lanes * (full + 2 * width),
            transcendentals=pairs * reqs * lanes * keys,
        ),
        name="attend",
    )(origins, prefix_len, *args)


def shards(
    hidden_in,
    kv_down,
    latent_gain,
    q_nope,
    q_rope,
    absorb_k,
    absorb_v,
    store,
    page_owner,
    page_slot,
    prefix_len,
):
    rows = hidden_in.shape[0]
    reqs = prefix_len.shape[0]
    new_len = rows // reqs
    kv_rank = latent_gain.shape[0]
    lat_width = kv_down.shape[1]
    nope_width = absorb_k.shape[1]
    rope_width = lat_width - kv_rank
    page = store.shape[1]
    dp_size = lax.axis_size("dp")
    tp_size = lax.axis_size("tp")
    z = lax.axis_index("tp")
    split = page // tp_size
    cols = kv_rank // LANES

    place = jnp.stack([z ^ i for i in range(tp_size)]).astype(jnp.int32)
    origins = ((z + jnp.arange(tp_size, dtype=jnp.int32)) % tp_size).astype(jnp.int32)
    own_rows = rows // tp_size
    token = z * own_rows + jnp.arange(own_rows, dtype=jnp.int32)
    position = jnp.where(token // new_len == 0, prefix_len[0], prefix_len[1]) + token % new_len
    piece = lax.dynamic_slice_in_dim(store, z * split, split, axis=1)

    def swap(given, far):
        return lax.ppermute(given, "tp", [(i, i ^ far) for i in range(tp_size)])

    want, pick = plan(page_owner[:, :, 0], page_slot, dp_size)
    asked = lax.all_to_all(want, "dp", split_axis=0, concat_axis=0, tiled=True)

    reply = gather_pages(asked, piece)
    reply, hidden_in, place, position = lax.optimization_barrier(
        (reply, hidden_in, place, position)
    )
    fetched = lax.all_to_all(reply, "dp", split_axis=0, concat_axis=0, tiled=True)

    cosine, sine = turn_tables(position, rope_width // 2)
    gain = latent_gain[None, :]
    kept, *gives = deal(place, hidden_in, kv_down.T, tp_size)
    got = [swap(given, i + 1) for i, given in enumerate(gives)]
    fresh = finish_latents(kept, gain, cosine, sine, got)
    fetched, fresh, q_nope = lax.optimization_barrier((fetched, fresh, q_nope))

    query = queries(q_nope, q_rope, absorb_k)
    attention = functools.partial(
        attend,
        query,
        origins=origins,
        prefix_len=prefix_len,
        factor=math.log2(math.e) / math.sqrt(nope_width + rope_width),
        page=page,
        split=split,
    )
    up = [(i, (i + 1) % tp_size) for i in range(tp_size)]
    down = [(i, (i - 1) % tp_size) for i in range(tp_size)]
    own = select_pages(pick, fetched.reshape(2 * dp_size, split, lat_width), fresh, cols)
    right, left = lax.ppermute(own, "tp", up), lax.ppermute(own, "tp", down)
    blocks, steps, state = [[right], [left], [own]], (tp_size - 1, 1, 0), None
    seen = [(0, own), (tp_size - 1, right), (1, left)]
    for far in range(2, tp_size // 2):
        next_right = lax.ppermute(right, "tp", up)
        next_left = lax.ppermute(left, "tp", down)
        state = attention(blocks=blocks, steps=steps, state=state)
        right, state = lax.optimization_barrier((next_right, state))
        left = next_left
        blocks, steps = [[right], [left]], (tp_size - far, far)
        seen += [(tp_size - far, right), (far, left)]
    cut = cols * LANES
    last = [lax.ppermute(right[:cut], "tp", up), lax.ppermute(left[cut:], "tp", down)]
    state = attention(blocks=blocks, steps=steps, state=state)
    attn_out, turned = attention(
        blocks=[last],
        steps=(tp_size // 2,),
        state=state,
        absorb_v=absorb_v,
        seen=tuple(seen),
    )
    return attn_out, turned.T


def solution(mesh):
    placed = (
        P("dp", "tp"),
        P("tp", None),
        P(),
        P("dp", "tp"),
        P("dp", "tp"),
        P("tp", None, None),
        P("tp", None, None),
        P("dp", None, None),
        P("dp", None, None),
        P("dp", None),
        P("dp"),
    )
    return jax.shard_map(
        shards,
        mesh=mesh,
        in_specs=placed,
        out_specs=(P("dp", "tp"), P("dp", None)),
        check_vma=False,
    )
```

time: 194 us -> 94.7 us (0.49)
  waiting for transfers between devices: 70.5 us -> 10 us
  local copies, waits for them, and re-layouts: 43 us -> 5.99 us
  starting transfers between devices: 6.86 us -> 42.8 us
  Pallas kernels: 0 us -> 33.1 us
  matrix products: 29.2 us -> 0 us
  other arithmetic: 15.8 us -> 1.42 us
  between operations: 14.2 us -> 0.9 us
  blocking collectives: 12.9 us -> 0 us
    psum x1 -> x0, waiting for transfers between devices: 70.5 us -> none  [shards(): raw_latent = lax.psum(raw_latent, 'tp')]
    pallas_call x0 -> x10, Pallas kernels: none -> 33.1 us  [the longest x4 26.1 us: attend(): pl.pallas_call(functools.partial(attend_body, pieces=tuple((len(parts) fo...]
    ppermute x0 -> x15, starting transfers between devices: none -> 29.4 us  [the longest x7 16.3 us: swap(): return lax.ppermute(given, 'tp', [(i, i ^ far) for i in range(tp_size)])]
    dot_general x7 -> x0, matrix products: 29.2 us -> none  [the longest x2 18.1 us: attend(): jnp.einsum('thc,hcv->thv', lat_out, absorb_v, preferred_element_type=jnp....]
    all_to_all x1 -> x0, blocking collectives: 12.9 us -> none  [shards(): lax.all_to_all(want_table, 'dp', split_axis=0, concat_axis=0, tiled=True)]
    while x14 -> x0, local copies, waits for them, and re-layouts: 10.6 us -> none  [the longest x2 7.13 us: shards(): lax.map(attend, (q_nope.reshape(reqs_dev, new_len, heads_dev, nope_width)...]
    gather x2 -> x0, local copies, waits for them, and re-layouts: 10.5 us -> none  [the longest x1 5.64 us: shards(): reply_pages = store[asked_ids]]
    ppermute x0 -> x15, waiting for transfers between devices: none -> 8.37 us  [the longest x7 5.05 us: swap(): return lax.ppermute(given, 'tp', [(i, i ^ far) for i in range(tp_size)])]
  transfers between devices with their start and end apart: 2 -> 17, of which waited for: 1 -> 5; matrix products, arithmetic and copies ran while one was open for 8% -> 4% of each run, Pallas kernels for 0% -> 21%
where the time goes in v2:
time: 94.7 us; the launch traced here: 94.3 us
  starting transfers between devices  42.8 us (45%)
  Pallas kernels  33.1 us (35%)
  waiting for transfers between devices  10 us (11%)
  local copies, waits for them, and re-layouts  5.99 us (6%)
  other arithmetic  1.42 us (1%)
    pallas_call x4, Pallas kernels, attend(): pl.pallas_call(functools.partial(attend_body, pieces=tuple((len(parts) fo...  26.1 us
    ppermute x7, starting transfers between devices, swap(): return lax.ppermute(given, 'tp', [(i, i ^ far) for i in range(tp_size)])  16.3 us
    all_to_all x1, starting transfers between devices, shards(): asked = lax.all_to_all(want, 'dp', split_axis=0, concat_axis=0, tiled=True)  7.62 us
    all_to_all x1, starting transfers between devices, shards(): lax.all_to_all(reply, 'dp', split_axis=0, concat_axis=0, tiled=True)  5.79 us
    ppermute x2, starting transfers between devices, shards(): next_left = lax.ppermute(left, 'tp', down)  5.69 us
    ppermute x7, waiting for transfers between devices, swap(): return lax.ppermute(given, 'tp', [(i, i ^ far) for i in range(tp_size)])  5.05 us
    ppermute x1, starting transfers between devices, shards(): lax.ppermute(left[cut:], 'tp', down)  3.51 us
    unnamed x18, local copies, waits for them, and re-layouts  3.48 us
  transfers between devices with their start and end apart: 17, of which 5 were waited for; matrix products, arithmetic and copies ran while one was open for 4% of the time, Pallas kernels for 21%

profile of v2, /device:TPU:6, one launch (start us, length us, event | category | flops | bytes accessed | tf_op | source)
XLA Modules:
  0.0 94.3 jit_solution(1209720157873100592)
XLA Ops:
  0.7 1.9 %plan.1 = (s32[32,1,2]{2,1,0:T(1,128)}, s32[32]{0:T(128)}) custom-call(s32[2,16]{1,0:T(2,128)} %bitcast.18, s32[2,16]{1,0:T(2,128)} %slot_ref.1), custom_call_target="tpu_custom_call" | custom-call | tf_op jit(solution)/shard_map/plan/pallas_call | solution.py:104
  2.6 7.6 %all-to-all-start = ((s32[32,1,2]{2,1,0:T(1,128)}), s32[32,1,2]{2,1,0:T(1,128)S(1)}, u32[]{:S(2)}, u32[]{:S(2)}) async-start(s32[32,1,2]{2,1,0:T(1,128)} %get-tuple-element.33), calls=%async_computation | async-start | bytes 32768 | tf_op jit(solution)/shard_map/all_to_all | solution.py:435
  10.2 1.3 %fusion.2 = (s32[1]{0:T(128)}, s32[1]{0:T(128)}) fusion(s32[2]{0:T(128)} %refs_1_.7), kind=kLoop, calls=%fused_computation.15 | loop fusion | bytes 16 | tf_op jit(solution)/shard_map/slice | solution.py:428
  11.6 1.1 %constant_dynamic-slice_fusion.pages_ref = bf16[48,8,576]{2,1,0:T(8,128)(2,1)S(1)} fusion(bf16[48,64,576]{2,1,0:T(8,128)(2,1)} %param.18, s32[]{:T(128)S(6)} %select_n.26), kind=kLoop, calls=%fused_computation.14 | loop fusion | bytes 884740 | tf_op jit(solution)/shard_map/dynamic_slice | solution.py:429
  12.6 1.3 %fusion = s32[32]{0:T(128)S(1)} fusion(s32[]{:T(128)} %bitcast.10, s32[]{:T(128)} %bitcast.9, s32[]{:T(128)S(6)} %mul.20), kind=kLoop, calls=%fused_computation.11 | loop fusion | flops 736 | bytes 140 | tf_op jit(solution)/shard_map/add | solution.py:428
  14.0 1.6 %all-to-all-done.ids_ref = s32[32,1,2]{2,1,0:T(1,128)S(1)} async-done(((s32[32,1,2]{2,1,0:T(1,128)}), s32[32,1,2]{2,1,0:T(1,128)S(1)}, u32[]{:S(2)}, u32[]{:S(2)}) %all-to-all-start) | async-done | bytes 288 | tf_op jit(solution)/shard_map/all_to_all | solution.py:435
  15.6 1.8 %gather_pages.1 = bf16[32,2,8,576]{3,2,1,0:T(8,128)(2,1)} custom-call(s32[32,1,2]{2,1,0:T(1,128)S(1)} %all-to-all-done.ids_ref, bf16[48,8,576]{2,1,0:T(8,128)(2,1)S(1)} %constant_dynamic-slice_fusion.pages_ref), custom_call_target="tpu_custom_call" | custom-call | tf_op jit(solution)/shard_map/gather_pages/pallas_call | solution.py:124
  17.4 5.8 %all-to-all-start.1 = ((bf16[32,2,8,576]{3,2,1,0:T(8,128)(2,1)}), bf16[32,2,8,576]{3,2,1,0:T(8,128)(2,1)S(1)}, u32[]{:S(2)}, u32[]{:S(2)}) async-start(bf16[32,2,8,576]{3,2,1,0:T(8,128)(2,1)} %gather_pages.1), calls=%async_computation.1 | async-start | bytes 1310720 | tf_op jit(solution)/shard_map/all_to_all | solution.py:441
  23.2 1.2 %copy-done.3 = bf16[896,576]{0,1:T(8,128)(2,1)S(1)} copy-done((bf16[896,576]{0,1:T(8,128)(2,1)S(1)}, bf16[896,576]{0,1:T(8,128)(2,1)}, u32[]{:S(2)}) %copy-start.3) | copy-done | bytes 1032216
  24.4 1.0 %copy-done.5 = bf16[256,896]{1,0:T(8,128)(2,1)S(1)} copy-done((bf16[256,896]{1,0:T(8,128)(2,1)S(1)}, bf16[256,896]{1,0:T(8,128)(2,1)}, u32[]{:S(2)}) %copy-start.5) | copy-done | bytes 458776
  25.4 1.2 %deal.1 = (f32[32,576]{1,0:T(8,128)S(1)}, bf16[32,576]{1,0:T(8,128)(2,1)S(1)}, bf16[32,576]{1,0:T(8,128)(2,1)S(1)}, bf16[32,576]{1,0:T(8,128)(2,1)S(1)}, bf16[32...) custom-call(s32[8]{0:T(128)S(1)} %stack.35.place_ref, ...), custom_call_target="tpu_custom_call" | custom-call | tf_op jit(solution)/shard_map/deal/pallas_call | solution.py:42
  26.6 2.0 %collective-permute-start = (bf16[32,576]{1,0:T(8,128)(2,1)S(1)}, bf16[32,576]{1,0:T(8,128)(2,1)S(1)}, u32[]{:S(2)}, u32[]{:S(2)}) collective-permute-start(bf16[32,576]{1,0:T(8,128)(2,1)S(1)} %get-tuple-element.39), channel_id=1, source_target_pairs={{0,1},{1,0},{2,3},{3,2},{4,5},{5,4},{6,7},{7,6},{8,9},{9,8},{10,11... | collective-permute-start | bytes 110600 | tf_op jit(solution)/shard_map/ppermute | solution.py:432
  28.6 3.3 %collective-permute-start.1 = (bf16[32,576]{1,0:T(8,128)(2,1)S(1)}, bf16[32,576]{1,0:T(8,128)(2,1)S(1)}, u32[]{:S(2)}, u32[]{:S(2)}) collective-permute-start(bf16[32,576]{1,0:T(8,128)(2,1)S(1)} %get-tuple-element.40), channel_id=1, source_target_pairs={{0,2},{1,3},{2,0},{3,1},{4,6},{5,7},{6,4},{7,5},{8,10},{9,11},{10,... | collective-permute-start | bytes 110600 | tf_op jit(solution)/shard_map/ppermute | solution.py:432
  31.9 6.4 %collective-permute-start.3 = (bf16[32,576]{1,0:T(8,128)(2,1)S(1)}, bf16[32,576]{1,0:T(8,128)(2,1)S(1)}, u32[]{:S(2)}, u32[]{:S(2)}) collective-permute-start(bf16[32,576]{1,0:T(8,128)(2,1)S(1)} %get-tuple-element.42), channel_id=1, source_target_pairs={{0,4},{1,5},{2,6},{3,7},{4,0},{5,1},{6,2},{7,3},{8,12},{9,13},{10,... | collective-permute-start | bytes 110600 | tf_op jit(solution)/shard_map/ppermute | solution.py:432
  38.3 4.6 %collective-permute-start.5 = (bf16[32,576]{1,0:T(8,128)(2,1)S(1)}, bf16[32,576]{1,0:T(8,128)(2,1)S(1)}, u32[]{:S(2)}, u32[]{:S(2)}) collective-permute-start(bf16[32,576]{1,0:T(8,128)(2,1)S(1)} %get-tuple-element.44), channel_id=1, source_target_pairs={{0,6},{1,7},{2,4},{3,5},{4,2},{5,3},{6,0},{7,1},{8,14},{9,15},{10,... | collective-permute-start | bytes 110600 | tf_op jit(solution)/shard_map/ppermute | solution.py:432
  43.1 2.3 %collective-permute-done.4.rest_4_ = bf16[32,576]{1,0:T(8,128)(2,1)S(1)} collective-permute-done((bf16[32,576]{1,0:T(8,128)(2,1)S(1)}, bf16[32,576]{1,0:T(8,128)(2,1)S(1)}, u32[]{:S(2)}, u32[]{:S(2)}) %collective-permute-start.4) | collective-permute-done | bytes 36896 | tf_op jit(solution)/shard_map/ppermute | solution.py:432
  45.4 2.7 %collective-permute-done.6.rest_6_ = bf16[32,576]{1,0:T(8,128)(2,1)S(1)} collective-permute-done((bf16[32,576]{1,0:T(8,128)(2,1)S(1)}, bf16[32,576]{1,0:T(8,128)(2,1)S(1)}, u32[]{:S(2)}, u32[]{:S(2)}) %collective-permute-start.6) | collective-permute-done | bytes 36896 | tf_op jit(solution)/shard_map/ppermute | solution.py:432
  48.3 0.6 select_pages.1.refs_5_.refs_7_
  49.0 2.0 %collective-permute-start.7 = (bf16[1296,128]{1,0:T(8,128)(2,1)S(1)}, bf16[1296,128]{1,0:T(8,128)(2,1)S(1)}, u32[]{:S(2)}, u32[]{:S(2)}) collective-permute-start(bf16[1296,128]{1,0:T(8,128)(2,1)S(1)} %select_pages.1.refs_5_.refs_7_), channel_id=1, source_target_pairs={{0,1},{1,2},{2,3},{3,4},{4,5},{5,6},{6,7},{7,0},{8,9},{9,10},{10,1... | collective-permute-start | bytes 995336 | tf_op jit(solution)/shard_map/ppermute | solution.py:463
  51.0 1.3 %collective-permute-start.9 = (bf16[1296,128]{1,0:T(8,128)(2,1)S(1)}, bf16[1296,128]{1,0:T(8,128)(2,1)S(1)}, u32[]{:S(2)}, u32[]{:S(2)}) collective-permute-start(bf16[1296,128]{1,0:T(8,128)(2,1)S(1)} %select_pages.1.refs_5_.refs_7_), channel_id=1, source_target_pairs={{0,7},{1,0},{2,1},{3,2},{4,3},{5,4},{6,5},{7,6},{8,15},{9,8},{10,9... | collective-permute-start | bytes 995336 | tf_op jit(solution)/shard_map/ppermute | solution.py:463
  52.3 1.2 %copy-done.2 = bf16[256,2048]{1,0:T(8,128)(2,1)S(1)} copy-done((bf16[256,2048]{1,0:T(8,128)(2,1)S(1)}, bf16[256,2048]{1,0:T(8,128)(2,1)}, u32[]{:S(2)}) %copy-start.2) | copy-done | bytes 1048600
  53.5 1.3 %queries.1.refs_2_ = bf16[8,2,640,256]{3,2,1,0:T(8,128)(2,1)S(1)} custom-call(bf16[256,2048]{1,0:T(8,128)(2,1)S(1)} %copy-done.2, bf16[256,1024]{1,0:T(8,128)(2,1)S(1)} %copy-done.4, bf16[16,128,512]{2,1,0:T(8,128)(2,1)S(1)} %copy-done), custom_call_target="tpu_custom_call" | custom-call | tf_op jit(solution)/shard_map/queries/pallas_call | solution.py:206
  54.9 3.0 %collective-permute-done.7.refs_3_.refs_8_ = bf16[1296,128]{1,0:T(8,128)(2,1)S(1)} collective-permute-done((bf16[1296,128]{1,0:T(8,128)(2,1)S(1)}, bf16[1296,128]{1,0:T(8,128)(2,1)S(1)}, u32[]{:S(2)}, u32[]{:S(2)}) %collective-permute-start.7) | collective-permute-done | bytes 331808 | tf_op jit(solution)/shard_map/ppermute | solution.py:463
  57.9 0.5 collective-permute-start.8
  58.4 0.3 collective-permute-done.9.refs_4_.refs_9_
  58.6 2.5 %collective-permute-start.11 = (bf16[1296,128]{1,0:T(8,128)(2,1)S(1)}, bf16[1296,128]{1,0:T(8,128)(2,1)S(1)}, u32[]{:S(2)}, u32[]{:S(2)}) collective-permute-start(bf16[1296,128]{1,0:T(8,128)(2,1)S(1)} %collective-permute-done.9.refs_4_.refs_9_), channel_id=1, source_target_pairs={{0,7},{1,0},{2,1},{3,2},{4,3},{5,4},{6,5},{7,6},{8,15},{9,8},{10,9... | collective-permute-start | bytes 995336 | tf_op jit(solution)/shard_map/ppermute | solution.py:468
  61.1 7.0 %attend.4 = (bf16[8,2,512,256]{3,2,1,0:T(8,128)(2,1)S(1)}, f32[8,2,8,256]{3,2,1,0:T(8,128)S(1)}) custom-call(s32[8]{0:T(128)S(1)} %and_select_fusion.2.refs_0_, s32[2]{0:T(128)S(1)} %copy-done.6, bf16[8,2,640,256]{3,2,1,0:T(8,128)(2,1)S(1)} %queries.1.refs_2_, bf16[1296,128]{1,0:T(8,128)(2,1)S(1)} %collective-permute-done.7.refs_3_.refs_8_, ...), custom_call_target="tpu_custom_call" | custom-call | flops 3623878656 | bytes 13631488 | tf_op jit(solution)/shard_map/attend/pallas_call | solution.py:364
  68.2 3.2 %collective-permute-start.13 = (bf16[1296,128]{1,0:T(8,128)(2,1)S(1)}, bf16[1296,128]{1,0:T(8,128)(2,1)S(1)}, u32[]{:S(2)}, u32[]{:S(2)}) collective-permute-start(bf16[1296,128]{1,0:T(8,128)(2,1)S(1)} %collective-permute-done.11.refs_4_.refs_11_), channel_id=1, source_target_pairs={{0,7},{1,0},{2,1},{3,2},{4,3},{5,4},{6,5},{7,6},{8,15},{9,8},{10,9... | collective-permute-start | bytes 995336 | tf_op jit(solution)/shard_map/ppermute | solution.py:468
  71.4 5.3 %attend.5 = (bf16[8,2,512,256]{3,2,1,0:T(8,128)(2,1)S(1)}, f32[8,2,8,256]{3,2,1,0:T(8,128)S(1)}) custom-call(s32[8]{0:T(128)S(1)} %and_select_fusion.2.refs_0_, s32[2]{0:T(128)S(1)} %copy-done.6, bf16[8,2,640,256]{3,2,1,0:T(8,128)(2,1)S(1)} %queries.1.refs_2_, ...), custom_call_target="tpu_custom_call", output_to_operand_aliasing={{0}: (5, {}), {1}: (6, {})} | custom-call | flops 2415919104 | bytes 13631488 | tf_op jit(solution)/shard_map/attend/pallas_call | solution.py:364
  76.9 3.5 %collective-permute-start.14 = (bf16[784,128]{1,0:T(8,128)(2,1)S(1)}, bf16[784,128]{1,0:T(8,128)(2,1)S(1)}, u32[]{:S(2)}, u32[]{:S(2)}) collective-permute-start(bf16[784,128]{1,0:T(8,128)(2,1)S(1)} %slice.16), channel_id=1, source_target_pairs={{0,7},{1,0},{2,1},{3,2},{4,3},{5,4},{6,5},{7,6},{8,15},{9,8},{10,9... | collective-permute-start | bytes 602120 | tf_op jit(solution)/shard_map/ppermute | solution.py:475
  80.4 5.3 %attend.6 = (bf16[8,2,512,256]{3,2,1,0:T(8,128)(2,1)S(1)}, f32[8,2,8,256]{3,2,1,0:T(8,128)S(1)}) custom-call(s32[8]{0:T(128)S(1)} %and_select_fusion.2.refs_0_, s32[2]{0:T(128)S(1)} %copy-done.6, bf16[8,2,640,256]{3,2,1,0:T(8,128)(2,1)S(1)} %queries.1.refs_2_, ...), custom_call_target="tpu_custom_call", output_to_operand_aliasing={{0}: (5, {}), {1}: (6, {})} | custom-call | flops 2415919104 | bytes 13631488 | tf_op jit(solution)/shard_map/attend/pallas_call | solution.py:364
  85.8 8.5 %attend.7 = (bf16[256,2048]{1,0:T(8,128)(2,1)}, bf16[576,256]{1,0:T(8,128)(2,1)}) custom-call(s32[8]{0:T(128)S(1)} %and_select_fusion.2.refs_0_, s32[2]{0:T(128)S(1)} %copy-done.6, bf16[8,2,640,256]{3,2,1,0:T(8,128)(2,1)S(1)} %queries.1.refs_2_, bf16[512,128]{1,0:T(8,128)(2,1)S(1)} %collective-permute-done.12.refs_3_, ...), custom_call_target="tpu_custom_call" | custom-call | flops 2415919104 | bytes 13631488 | tf_op jit(solution)/shard_map/attend/pallas_call | solution.py:364
  (40 shorter events, 0.7 us)
Async XLA Ops:
  0.6 47.5 %copy-start.7 = (f32[512]{0:T(512)S(1)}, f32[512]{0:T(512)}, u32[]{:S(2)}) copy-start(f32[512]{0:T(512)} %param.13) | copy-start | bytes 6148
  0.6 51.7 %copy-start.4 = (bf16[256,1024]{1,0:T(8,128)(2,1)S(1)}, bf16[256,1024]{1,0:T(8,128)(2,1)}, u32[]{:S(2)}) copy-start(bf16[256,1024]{1,0:T(8,128)(2,1)} %rope_ref.1) | copy-start | bytes 1572868
  0.7 51.7 %copy-start = (bf16[16,128,512]{2,1,0:T(8,128)(2,1)S(1)}, bf16[16,128,512]{2,1,0:T(8,128)(2,1)}, u32[]{:S(2)}) copy-start(bf16[16,128,512]{2,1,0:T(8,128)(2,1)} %absorb_ref.1) | copy-start | bytes 6291460
  2.6 45.7 %copy-start.8 = (s32[32]{0:T(128)S(1)}, s32[32]{0:T(128)}, u32[]{:S(2)}) copy-start(s32[32]{0:T(128)} %get-tuple-element.47.pick_ref) | copy-start | bytes 388
  2.6 13.0 %all-to-all-start = ((s32[32,1,2]{2,1,0:T(1,128)}), s32[32,1,2]{2,1,0:T(1,128)S(1)}, u32[]{:S(2)}, u32[]{:S(2)}) async-start(s32[32,1,2]{2,1,0:T(1,128)} %get-tuple-element.33), calls=%async_computation | async-start | bytes 32768 | tf_op jit(solution)/shard_map/all_to_all | solution.py:435
  17.4 30.9 %all-to-all-start.1 = ((bf16[32,2,8,576]{3,2,1,0:T(8,128)(2,1)}), bf16[32,2,8,576]{3,2,1,0:T(8,128)(2,1)S(1)}, u32[]{:S(2)}, u32[]{:S(2)}) async-start(bf16[32,2,8,576]{3,2,1,0:T(8,128)(2,1)} %gather_pages.1), calls=%async_computation.1 | async-start | bytes 1310720 | tf_op jit(solution)/shard_map/all_to_all | solution.py:441
  23.2 1.2 %copy-start.3 = (bf16[896,576]{0,1:T(8,128)(2,1)S(1)}, bf16[896,576]{0,1:T(8,128)(2,1)}, u32[]{:S(2)}) copy-start(bf16[896,576]{0,1:T(8,128)(2,1)} %param.12) | copy-start | bytes 3096580
  24.4 1.0 %copy-start.5 = (bf16[256,896]{1,0:T(8,128)(2,1)S(1)}, bf16[256,896]{1,0:T(8,128)(2,1)}, u32[]{:S(2)}) copy-start(bf16[256,896]{1,0:T(8,128)(2,1)} %hidden_ref) | copy-start | bytes 1376260
  26.6 11.7 %collective-permute-start = (bf16[32,576]{1,0:T(8,128)(2,1)S(1)}, bf16[32,576]{1,0:T(8,128)(2,1)S(1)}, u32[]{:S(2)}, u32[]{:S(2)}) collective-permute-start(bf16[32,576]{1,0:T(8,128)(2,1)S(1)} %get-tuple-element.39), channel_id=1, source_target_pairs={{0,1},{1,0},{2,3},{3,2},{4,5},{5,4},{6,7},{7,6},{8,9},{9,8},{10,11... | collective-permute-start | bytes 110600 | tf_op jit(solution)/shard_map/ppermute | solution.py:432
  28.6 14.3 %collective-permute-start.1 = (bf16[32,576]{1,0:T(8,128)(2,1)S(1)}, bf16[32,576]{1,0:T(8,128)(2,1)S(1)}, u32[]{:S(2)}, u32[]{:S(2)}) collective-permute-start(bf16[32,576]{1,0:T(8,128)(2,1)S(1)} %get-tuple-element.40), channel_id=1, source_target_pairs={{0,2},{1,3},{2,0},{3,1},{4,6},{5,7},{6,4},{7,5},{8,10},{9,11},{10,... | collective-permute-start | bytes 110600 | tf_op jit(solution)/shard_map/ppermute | solution.py:432
  31.9 11.2 %collective-permute-start.2 = (bf16[32,576]{1,0:T(8,128)(2,1)S(1)}, bf16[32,576]{1,0:T(8,128)(2,1)S(1)}, u32[]{:S(2)}, u32[]{:S(2)}) collective-permute-start(bf16[32,576]{1,0:T(8,128)(2,1)S(1)} %get-tuple-element.41), channel_id=1, source_target_pairs={{0,3},{1,2},{2,1},{3,0},{4,7},{5,6},{6,5},{7,4},{8,11},{9,10},{10,... | collective-permute-start | bytes 110600 | tf_op jit(solution)/shard_map/ppermute | solution.py:432
  31.9 11.2 %collective-permute-start.3 = (bf16[32,576]{1,0:T(8,128)(2,1)S(1)}, bf16[32,576]{1,0:T(8,128)(2,1)S(1)}, u32[]{:S(2)}, u32[]{:S(2)}) collective-permute-start(bf16[32,576]{1,0:T(8,128)(2,1)S(1)} %get-tuple-element.42), channel_id=1, source_target_pairs={{0,4},{1,5},{2,6},{3,7},{4,0},{5,1},{6,2},{7,3},{8,12},{9,13},{10,... | collective-permute-start | bytes 110600 | tf_op jit(solution)/shard_map/ppermute | solution.py:432
  38.3 7.1 %collective-permute-start.4 = (bf16[32,576]{1,0:T(8,128)(2,1)S(1)}, bf16[32,576]{1,0:T(8,128)(2,1)S(1)}, u32[]{:S(2)}, u32[]{:S(2)}) collective-permute-start(bf16[32,576]{1,0:T(8,128)(2,1)S(1)} %get-tuple-element.43), channel_id=1, source_target_pairs={{0,5},{1,4},{2,7},{3,6},{4,1},{5,0},{6,3},{7,2},{8,13},{9,12},{10,... | collective-permute-start | bytes 110600 | tf_op jit(solution)/shard_map/ppermute | solution.py:432
  38.3 7.1 %collective-permute-start.5 = (bf16[32,576]{1,0:T(8,128)(2,1)S(1)}, bf16[32,576]{1,0:T(8,128)(2,1)S(1)}, u32[]{:S(2)}, u32[]{:S(2)}) collective-permute-start(bf16[32,576]{1,0:T(8,128)(2,1)S(1)} %get-tuple-element.44), channel_id=1, source_target_pairs={{0,6},{1,7},{2,4},{3,5},{4,2},{5,3},{6,0},{7,1},{8,14},{9,15},{10,... | collective-permute-start | bytes 110600 | tf_op jit(solution)/shard_map/ppermute | solution.py:432
  42.9 5.2 %collective-permute-start.6 = (bf16[32,576]{1,0:T(8,128)(2,1)S(1)}, bf16[32,576]{1,0:T(8,128)(2,1)S(1)}, u32[]{:S(2)}, u32[]{:S(2)}) collective-permute-start(bf16[32,576]{1,0:T(8,128)(2,1)S(1)} %get-tuple-element.45), channel_id=1, source_target_pairs={{0,7},{1,6},{2,5},{3,4},{4,3},{5,2},{6,1},{7,0},{8,15},{9,14},{10,... | collective-permute-start | bytes 110600 | tf_op jit(solution)/shard_map/ppermute | solution.py:432
  49.0 8.9 %collective-permute-start.7 = (bf16[1296,128]{1,0:T(8,128)(2,1)S(1)}, bf16[1296,128]{1,0:T(8,128)(2,1)S(1)}, u32[]{:S(2)}, u32[]{:S(2)}) collective-permute-start(bf16[1296,128]{1,0:T(8,128)(2,1)S(1)} %select_pages.1.refs_5_.refs_7_), channel_id=1, source_target_pairs={{0,1},{1,2},{2,3},{3,4},{4,5},{5,6},{6,7},{7,0},{8,9},{9,10},{10,1... | collective-permute-start | bytes 995336 | tf_op jit(solution)/shard_map/ppermute | solution.py:463
  51.0 7.7 %collective-permute-start.9 = (bf16[1296,128]{1,0:T(8,128)(2,1)S(1)}, bf16[1296,128]{1,0:T(8,128)(2,1)S(1)}, u32[]{:S(2)}, u32[]{:S(2)}) collective-permute-start(bf16[1296,128]{1,0:T(8,128)(2,1)S(1)} %select_pages.1.refs_5_.refs_7_), channel_id=1, source_target_pairs={{0,7},{1,0},{2,1},{3,2},{4,3},{5,4},{6,5},{7,6},{8,15},{9,8},{10,9... | collective-permute-start | bytes 995336 | tf_op jit(solution)/shard_map/ppermute | solution.py:463
  52.3 1.2 %copy-start.2 = (bf16[256,2048]{1,0:T(8,128)(2,1)S(1)}, bf16[256,2048]{1,0:T(8,128)(2,1)}, u32[]{:S(2)}) copy-start(bf16[256,2048]{1,0:T(8,128)(2,1)} %nope_ref) | copy-start | bytes 3145732
  53.5 7.6 %copy-start.6 = (s32[2]{0:T(128)S(1)}, s32[2]{0:T(128)}, u32[]{:S(2)}) copy-start(s32[2]{0:T(128)} %refs_1_.7) | copy-start | bytes 28
  57.9 10.2 %collective-permute-start.8 = (bf16[1296,128]{1,0:T(8,128)(2,1)S(1)}, bf16[1296,128]{1,0:T(8,128)(2,1)S(1)}, u32[]{:S(2)}, u32[]{:S(2)}) collective-permute-start(bf16[1296,128]{1,0:T(8,128)(2,1)S(1)} %collective-permute-done.7.refs_3_.refs_8_), channel_id=1, source_target_pairs={{0,1},{1,2},{2,3},{3,4},{4,5},{5,6},{6,7},{7,0},{8,9},{9,10},{10,1... | collective-permute-start | bytes 995336 | tf_op jit(solution)/shard_map/ppermute | solution.py:467
  58.6 9.6 %collective-permute-start.11 = (bf16[1296,128]{1,0:T(8,128)(2,1)S(1)}, bf16[1296,128]{1,0:T(8,128)(2,1)S(1)}, u32[]{:S(2)}, u32[]{:S(2)}) collective-permute-start(bf16[1296,128]{1,0:T(8,128)(2,1)S(1)} %collective-permute-done.9.refs_4_.refs_9_), channel_id=1, source_target_pairs={{0,7},{1,0},{2,1},{3,2},{4,3},{5,4},{6,5},{7,6},{8,15},{9,8},{10,9... | collective-permute-start | bytes 995336 | tf_op jit(solution)/shard_map/ppermute | solution.py:468
  68.1 8.6 %collective-permute-start.10 = (bf16[1296,128]{1,0:T(8,128)(2,1)S(1)}, bf16[1296,128]{1,0:T(8,128)(2,1)S(1)}, u32[]{:S(2)}, u32[]{:S(2)}) collective-permute-start(bf16[1296,128]{1,0:T(8,128)(2,1)S(1)} %collective-permute-done.8.refs_3_.refs_10_), channel_id=1, source_target_pairs={{0,1},{1,2},{2,3},{3,4},{4,5},{5,6},{6,7},{7,0},{8,9},{9,10},{10,1... | collective-permute-start | bytes 995336 | tf_op jit(solution)/shard_map/ppermute | solution.py:467
  68.2 8.7 %collective-permute-start.13 = (bf16[1296,128]{1,0:T(8,128)(2,1)S(1)}, bf16[1296,128]{1,0:T(8,128)(2,1)S(1)}, u32[]{:S(2)}, u32[]{:S(2)}) collective-permute-start(bf16[1296,128]{1,0:T(8,128)(2,1)S(1)} %collective-permute-done.11.refs_4_.refs_11_), channel_id=1, source_target_pairs={{0,7},{1,0},{2,1},{3,2},{4,3},{5,4},{6,5},{7,6},{8,15},{9,8},{10,9... | collective-permute-start | bytes 995336 | tf_op jit(solution)/shard_map/ppermute | solution.py:468
  76.8 9.0 %collective-permute-start.12 = (bf16[512,128]{1,0:T(8,128)(2,1)S(1)}, bf16[512,128]{1,0:T(8,128)(2,1)S(1)}, u32[]{:S(2)}, u32[]{:S(2)}) collective-permute-start(bf16[512,128]{1,0:T(8,128)(2,1)S(1)} %slice.14), channel_id=1, source_target_pairs={{0,1},{1,2},{2,3},{3,4},{4,5},{5,6},{6,7},{7,0},{8,9},{9,10},{10,1... | collective-permute-start | bytes 393224 | tf_op jit(solution)/shard_map/ppermute | solution.py:475
  76.9 8.9 %copy-start.1 = (bf16[16,512,128]{2,1,0:T(8,128)(2,1)S(1)}, bf16[16,512,128]{2,1,0:T(8,128)(2,1)}, u32[]{:S(2)}) copy-start(bf16[16,512,128]{2,1,0:T(8,128)(2,1)} %refs_14_.1) | copy-start | bytes 6291460
  76.9 8.8 %collective-permute-start.14 = (bf16[784,128]{1,0:T(8,128)(2,1)S(1)}, bf16[784,128]{1,0:T(8,128)(2,1)S(1)}, u32[]{:S(2)}, u32[]{:S(2)}) collective-permute-start(bf16[784,128]{1,0:T(8,128)(2,1)S(1)} %slice.16), channel_id=1, source_target_pairs={{0,7},{1,0},{2,1},{3,2},{4,3},{5,4},{6,5},{7,6},{8,15},{9,8},{10,9... | collective-permute-start | bytes 602120 | tf_op jit(solution)/shard_map/ppermute | solution.py:475

commit v3 on v2

--- a/solution.py
+++ b/solution.py
@@ -25,30 +25,25 @@
 SMALL = pltpu.CompilerParams(vmem_limit_bytes=4 << 20)
 
 
-def deal_body(place_ref, hidden_ref, down_ref, keep_ref, *rest):
-    part_ref = rest[-1]
-    part_ref[...] = lax.dot_general(
-        hidden_ref[...], down_ref[...], (((1,), (1,)), ((), ())), preferred_element_type=F32
-    )
+def deal_body(place_ref, part_ref, keep_ref, *gives):
     rows = keep_ref.shape[0]
     keep_ref[...] = part_ref[pl.ds(pl.multiple_of(place_ref[0] * rows, rows), rows), :]
-    for i, give_ref in enumerate(rest[:-1]):
+    for i, give_ref in enumerate(gives):
         other = pl.multiple_of(place_ref[1 + i] * rows, rows)
         give_ref[...] = part_ref[pl.ds(other, rows), :].astype(BF16)
 
 
-def deal(place, hidden, down, members):
-    rows, width = hidden.shape[0] // members, down.shape[0]
+def deal(place, part, members):
+    rows, width = part.shape[0] // members, part.shape[1]
     return pl.pallas_call(
         deal_body,
         out_shape=(jax.ShapeDtypeStruct((rows, width), F32),)
         + (jax.ShapeDtypeStruct((rows, width), BF16),) * (members - 1),
-        in_specs=[SMEM, VMEM, VMEM],
+        in_specs=[SMEM, VMEM],
         out_specs=(VMEM,) * members,
-        scratch_shapes=[pltpu.VMEM((hidden.shape[0], width), F32)],
         compiler_params=SMALL,
         name="deal",
-    )(place, hidden, down)
+    )(place, part)
 
 
 def finish_body(kept_ref, gain_ref, cos_ref, sin_ref, *rest):
@@ -288,16 +283,19 @@
         bias = bias_ref[r]
         return s + jnp.concatenate([bias, bias], axis=1)
 
-    def finish(r, k, s):
+    def soften(r, k, s):
         top = jnp.max(s, axis=0, keepdims=True)
         if not first:
             old_top = stat_in[k, r, 0:1, :]
             top = jnp.maximum(top, old_top)
         expo = jnp.exp2((s - top) * factor)
         total = jnp.sum(expo, axis=0, keepdims=True)
-        acc = jnp.dot(values_ref[r], expo.astype(BF16), preferred_element_type=F32)
+        return expo.astype(BF16), top, total
+
+    def finish(r, k, probs, top, total):
+        acc = jnp.dot(values_ref[r], probs, preferred_element_type=F32)
         if not first:
-            alpha = jnp.exp2((old_top - top) * factor)
+            alpha = jnp.exp2((stat_in[k, r, 0:1, :] - top) * factor)
             total = total + alpha * stat_in[k, r, 1:2, :]
             acc = acc + alpha * acc_in[k, r].astype(F32)
         if last:
@@ -329,11 +327,15 @@
             turned_ref[: full - LANES, own] = values_ref[r, :, len(blocks) * LANES :]
             turned_ref[full - LANES :, own] = new_ref[own, full - LANES :].T
     order = [(r, k) for r in range(reqs) for k in range(pairs)]
-    s = score(*order[0])
-    for i, (r, k) in enumerate(order):
-        following = score(*order[i + 1]) if i + 1 < len(order) else None
-        finish(r, k, s)
-        s = following
+    count = len(order)
+    scores, probs = {}, {}
+    for i in range(count + 2):
+        if i < count:
+            scores[i] = score(*order[i])
+        if 0 <= i - 1 < count:
+            probs[i - 1] = soften(*order[i - 1], scores.pop(i - 1))
+        if 0 <= i - 2 < count:
+            finish(*order[i - 2], *probs.pop(i - 2))
 
 
 def attend(
@@ -442,7 +444,8 @@
 
     cosine, sine = turn_tables(position, rope_width // 2)
     gain = latent_gain[None, :]
-    kept, *gives = deal(place, hidden_in, kv_down.T, tp_size)
+    part = jnp.dot(hidden_in, kv_down, preferred_element_type=F32)
+    kept, *gives = deal(place, part, tp_size)
     got = [swap(given, i + 1) for i, given in enumerate(gives)]
     fresh = finish_latents(kept, gain, cosine, sine, got)
     fetched, fresh, q_nope = lax.optimization_barrier((fetched, fresh, q_nope))
@@ -461,7 +464,9 @@
     down = [(i, (i - 1) % tp_size) for i in range(tp_size)]
     own = select_pages(pick, fetched.reshape(2 * dp_size, split, lat_width), fresh, cols)
     right, left = lax.ppermute(own, "tp", up), lax.ppermute(own, "tp", down)
-    blocks, steps, state = [[right], [left], [own]], (tp_size - 1, 1, 0), None
+    state = attention(blocks=[[own]], steps=(0,))
+    right, left, state = lax.optimization_barrier((right, left, state))
+    blocks, steps = [[right], [left]], (tp_size - 1, 1)
     seen = [(0, own), (tp_size - 1, right), (1, left)]
     for far in range(2, tp_size // 2):
         next_right = lax.ppermute(right, "tp", up)
@@ -471,7 +476,7 @@
         left = next_left
         blocks, steps = [[right], [left]], (tp_size - far, far)
         seen += [(tp_size - far, right), (far, left)]
-    cut = cols * LANES
+    cut = (2 * cols + 1) * 2 // 3 * LANES
     last = [lax.ppermute(right[:cut], "tp", up), lax.ppermute(left[cut:], "tp", down)]
     state = attention(blocks=blocks, steps=steps, state=state)
     attn_out, turned = attention(

time: 94.7 us -> 91.3 us (0.964)
  local copies, waits for them, and re-layouts: 5.99 us -> 4.13 us
  Pallas kernels: 33.1 us -> 31.3 us
  matrix products: 0 us -> 1.6 us
  waiting for transfers between devices: 10 us -> 8.59 us
    ppermute x2, waiting for transfers between devices: 3.3 us -> 0.01 us  [shards(): right, left = (lax.ppermute(own, 'tp', up), lax.ppermute(own, 'tp', down))]
    unnamed x18 -> x16, local copies, waits for them, and re-layouts: 3.48 us -> 1.62 us
    ppermute x2, waiting for transfers between devices: 0.01 us -> 1.7 us  [shards(): next_right = lax.ppermute(right, 'tp', up)]
    dot_general x0 -> x1, matrix products: none -> 1.6 us  [shards(): part = jnp.dot(hidden_in, kv_down, preferred_element_type=F32)]
    pallas_call x4 -> x5, Pallas kernels: 26.1 us -> 24.9 us  [attend(): pl.pallas_call(functools.partial(attend_body, pieces=tuple((len(parts) fo...]
  transfers between devices with their start and end apart: 17 -> 17, of which waited for: 5 -> 6; matrix products, arithmetic and copies ran while one was open for 4% -> 6% of each run, Pallas kernels for 21% -> 21%
where the time goes in v3:
time: 91.3 us; the launch traced here: 91 us
  starting transfers between devices  43 us (47%)
  Pallas kernels  31.3 us (34%)
  waiting for transfers between devices  8.59 us (9%)
  local copies, waits for them, and re-layouts  4.13 us (5%)
  matrix products  1.6 us (2%)
  other arithmetic  1.42 us (2%)
    pallas_call x5, Pallas kernels, attend(): pl.pallas_call(functools.partial(attend_body, pieces=tuple((len(parts) fo...  24.9 us
    ppermute x7, starting transfers between devices, swap(): return lax.ppermute(given, 'tp', [(i, i ^ far) for i in range(tp_size)])  16.3 us
    all_to_all x1, starting transfers between devices, shards(): asked = lax.all_to_all(want, 'dp', split_axis=0, concat_axis=0, tiled=True)  7.62 us
    all_to_all x1, starting transfers between devices, shards(): lax.all_to_all(reply, 'dp', split_axis=0, concat_axis=0, tiled=True)  5.8 us
    ppermute x2, starting transfers between devices, shards(): next_left = lax.ppermute(left, 'tp', down)  5.46 us
    ppermute x7, waiting for transfers between devices, swap(): return lax.ppermute(given, 'tp', [(i, i ^ far) for i in range(tp_size)])  5.05 us
    ppermute x1, starting transfers between devices, shards(): lax.ppermute(left[cut:], 'tp', down)  3.51 us
    ppermute x2, starting transfers between devices, shards(): right, left = (lax.ppermute(own, 'tp', up), lax.ppermute(own, 'tp', down))  3.31 us
  transfers between devices with their start and end apart: 17, of which 6 were waited for; matrix products, arithmetic and copies ran while one was open for 6% of the time, Pallas kernels for 21%

profile of v3, /device:TPU:6, one launch (start us, length us, event | category | flops | bytes accessed | tf_op | source)
XLA Modules:
  0.0 91.0 jit_solution(505328172512435445)
XLA Ops:
  0.7 1.9 %plan.1 = (s32[32,1,2]{2,1,0:T(1,128)}, s32[32]{0:T(128)}) custom-call(s32[2,16]{1,0:T(2,128)} %bitcast.18, s32[2,16]{1,0:T(2,128)} %slot_ref.1), custom_call_target="tpu_custom_call" | custom-call | tf_op jit(solution)/shard_map/plan/pallas_call | solution.py:99
  2.6 7.6 %all-to-all-start = ((s32[32,1,2]{2,1,0:T(1,128)}), s32[32,1,2]{2,1,0:T(1,128)S(1)}, u32[]{:S(2)}, u32[]{:S(2)}) async-start(s32[32,1,2]{2,1,0:T(1,128)} %get-tuple-element.39), calls=%async_computation | async-start | bytes 32768 | tf_op jit(solution)/shard_map/all_to_all | solution.py:437
  10.3 1.3 %fusion.2 = (s32[1]{0:T(128)}, s32[1]{0:T(128)}) fusion(s32[2]{0:T(128)} %refs_1_.9), kind=kLoop, calls=%fused_computation.15 | loop fusion | bytes 16 | tf_op jit(solution)/shard_map/slice | solution.py:430
  11.6 1.1 %constant_dynamic-slice_fusion.pages_ref = bf16[48,8,576]{2,1,0:T(8,128)(2,1)S(1)} fusion(bf16[48,64,576]{2,1,0:T(8,128)(2,1)} %param.18, s32[]{:T(128)S(6)} %select_n.26), kind=kLoop, calls=%fused_computation.14 | loop fusion | bytes 884740 | tf_op jit(solution)/shard_map/dynamic_slice | solution.py:431
  12.7 1.3 %fusion = s32[32]{0:T(128)S(1)} fusion(s32[]{:T(128)} %bitcast.10, s32[]{:T(128)} %bitcast.9, s32[]{:T(128)S(6)} %mul.20), kind=kLoop, calls=%fused_computation.11 | loop fusion | flops 736 | bytes 140 | tf_op jit(solution)/shard_map/add | solution.py:430
  14.0 1.6 %all-to-all-done.ids_ref = s32[32,1,2]{2,1,0:T(1,128)S(1)} async-done(((s32[32,1,2]{2,1,0:T(1,128)}), s32[32,1,2]{2,1,0:T(1,128)S(1)}, u32[]{:S(2)}, u32[]{:S(2)}) %all-to-all-start) | async-done | bytes 288 | tf_op jit(solution)/shard_map/all_to_all | solution.py:437
  15.6 1.8 %gather_pages.1 = bf16[32,2,8,576]{3,2,1,0:T(8,128)(2,1)} custom-call(s32[32,1,2]{2,1,0:T(1,128)S(1)} %all-to-all-done.ids_ref, bf16[48,8,576]{2,1,0:T(8,128)(2,1)S(1)} %constant_dynamic-slice_fusion.pages_ref), custom_call_target="tpu_custom_call" | custom-call | tf_op jit(solution)/shard_map/gather_pages/pallas_call | solution.py:119
  17.4 5.8 %all-to-all-start.1 = ((bf16[32,2,8,576]{3,2,1,0:T(8,128)(2,1)}), bf16[32,2,8,576]{3,2,1,0:T(8,128)(2,1)S(1)}, u32[]{:S(2)}, u32[]{:S(2)}) async-start(bf16[32,2,8,576]{3,2,1,0:T(8,128)(2,1)} %gather_pages.1), calls=%async_computation.1 | async-start | bytes 1310720 | tf_op jit(solution)/shard_map/all_to_all | solution.py:443
  23.2 1.6 %fusion.3.part_ref = f32[256,576]{1,0:T(8,128)S(1)} fusion(bf16[256,896]{1,0:T(8,128)(2,1)} %param.11, bf16[896,576]{0,1:T(8,128)(2,1)S(1)} %copy-done), kind=kOutput, calls=%fused_computation.16 | convolution fusion | flops 264241152 | bytes 2080768 | tf_op jit(solution)/shard_map/dot_general | solution.py:447
  24.8 0.6 deal.1
  25.4 2.0 %collective-permute-start = (bf16[32,576]{1,0:T(8,128)(2,1)S(1)}, bf16[32,576]{1,0:T(8,128)(2,1)S(1)}, u32[]{:S(2)}, u32[]{:S(2)}) collective-permute-start(bf16[32,576]{1,0:T(8,128)(2,1)S(1)} %get-tuple-element.45), channel_id=1, source_target_pairs={{0,1},{1,0},{2,3},{3,2},{4,5},{5,4},{6,7},{7,6},{8,9},{9,8},{10,11... | collective-permute-start | bytes 110600 | tf_op jit(solution)/shard_map/ppermute | solution.py:434
  27.4 3.3 %collective-permute-start.1 = (bf16[32,576]{1,0:T(8,128)(2,1)S(1)}, bf16[32,576]{1,0:T(8,128)(2,1)S(1)}, u32[]{:S(2)}, u32[]{:S(2)}) collective-permute-start(bf16[32,576]{1,0:T(8,128)(2,1)S(1)} %get-tuple-element.46), channel_id=1, source_target_pairs={{0,2},{1,3},{2,0},{3,1},{4,6},{5,7},{6,4},{7,5},{8,10},{9,11},{10,... | collective-permute-start | bytes 110600 | tf_op jit(solution)/shard_map/ppermute | solution.py:434
  30.7 6.4 %collective-permute-start.3 = (bf16[32,576]{1,0:T(8,128)(2,1)S(1)}, bf16[32,576]{1,0:T(8,128)(2,1)S(1)}, u32[]{:S(2)}, u32[]{:S(2)}) collective-permute-start(bf16[32,576]{1,0:T(8,128)(2,1)S(1)} %get-tuple-element.48), channel_id=1, source_target_pairs={{0,4},{1,5},{2,6},{3,7},{4,0},{5,1},{6,2},{7,3},{8,12},{9,13},{10,... | collective-permute-start | bytes 110600 | tf_op jit(solution)/shard_map/ppermute | solution.py:434
  37.1 4.6 %collective-permute-start.5 = (bf16[32,576]{1,0:T(8,128)(2,1)S(1)}, bf16[32,576]{1,0:T(8,128)(2,1)S(1)}, u32[]{:S(2)}, u32[]{:S(2)}) collective-permute-start(bf16[32,576]{1,0:T(8,128)(2,1)S(1)} %get-tuple-element.50), channel_id=1, source_target_pairs={{0,6},{1,7},{2,4},{3,5},{4,2},{5,3},{6,0},{7,1},{8,14},{9,15},{10,... | collective-permute-start | bytes 110600 | tf_op jit(solution)/shard_map/ppermute | solution.py:434
  41.9 2.3 %collective-permute-done.4.rest_4_ = bf16[32,576]{1,0:T(8,128)(2,1)S(1)} collective-permute-done((bf16[32,576]{1,0:T(8,128)(2,1)S(1)}, bf16[32,576]{1,0:T(8,128)(2,1)S(1)}, u32[]{:S(2)}, u32[]{:S(2)}) %collective-permute-start.4) | collective-permute-done | bytes 36896 | tf_op jit(solution)/shard_map/ppermute | solution.py:434
  44.2 2.7 %collective-permute-done.6.rest_6_ = bf16[32,576]{1,0:T(8,128)(2,1)S(1)} collective-permute-done((bf16[32,576]{1,0:T(8,128)(2,1)S(1)}, bf16[32,576]{1,0:T(8,128)(2,1)S(1)}, u32[]{:S(2)}, u32[]{:S(2)}) %collective-permute-start.6) | collective-permute-done | bytes 36896 | tf_op jit(solution)/shard_map/ppermute | solution.py:434
  47.2 0.6 select_pages.1.refs_3_.refs_7_
  47.8 2.0 %collective-permute-start.7 = (bf16[1296,128]{1,0:T(8,128)(2,1)S(1)}, bf16[1296,128]{1,0:T(8,128)(2,1)S(1)}, u32[]{:S(2)}, u32[]{:S(2)}) collective-permute-start(bf16[1296,128]{1,0:T(8,128)(2,1)S(1)} %select_pages.1.refs_3_.refs_7_), channel_id=1, source_target_pairs={{0,1},{1,2},{2,3},{3,4},{4,5},{5,6},{6,7},{7,0},{8,9},{9,10},{10,1... | collective-permute-start | bytes 995336 | tf_op jit(solution)/shard_map/ppermute | solution.py:466
  49.8 1.3 %collective-permute-start.8 = (bf16[1296,128]{1,0:T(8,128)(2,1)S(1)}, bf16[1296,128]{1,0:T(8,128)(2,1)S(1)}, u32[]{:S(2)}, u32[]{:S(2)}) collective-permute-start(bf16[1296,128]{1,0:T(8,128)(2,1)S(1)} %select_pages.1.refs_3_.refs_7_), channel_id=1, source_target_pairs={{0,7},{1,0},{2,1},{3,2},{4,3},{5,4},{6,5},{7,6},{8,15},{9,8},{10,9... | collective-permute-start | bytes 995336 | tf_op jit(solution)/shard_map/ppermute | solution.py:466
  51.2 1.6 %copy-done.1 = bf16[16,128,512]{2,1,0:T(8,128)(2,1)S(1)} copy-done((bf16[16,128,512]{2,1,0:T(8,128)(2,1)S(1)}, bf16[16,128,512]{2,1,0:T(8,128)(2,1)}, u32[]{:S(2)}) %copy-start.1) | copy-done | bytes 2097176
  52.7 1.3 %queries.1.refs_2_ = bf16[8,2,640,256]{3,2,1,0:T(8,128)(2,1)S(1)} custom-call(bf16[256,2048]{1,0:T(8,128)(2,1)S(1)} %copy-done.3, bf16[256,1024]{1,0:T(8,128)(2,1)S(1)} %copy-done.4, bf16[16,128,512]{2,1,0:T(8,128)(2,1)S(1)} %copy-done.1), custom_call_target="tpu_custom_call" | custom-call | tf_op jit(solution)/shard_map/queries/pallas_call | solution.py:201
  54.1 2.9 %attend.5 = (bf16[8,2,512,256]{3,2,1,0:T(8,128)(2,1)S(1)}, f32[8,2,8,256]{3,2,1,0:T(8,128)S(1)}) custom-call(s32[8]{0:T(128)S(1)} %and_select_fusion.2.refs_0_, s32[2]{0:T(128)S(1)} %copy-done.5, bf16[8,2,640,256]{3,2,1,0:T(8,128)(2,1)S(1)} %queries.1.refs_2_, bf16[1296,128]{1,0:T(8,128)(2,1)S(1)} %select_pages.1.refs_3_.refs_7_), custom_call_target="tpu_custom_call" | custom-call | flops 1207959552 | bytes 13631488 | tf_op jit(solution)/shard_map/attend/pallas_call | solution.py:366
  57.0 0.9 %collective-permute-start.9 = (bf16[1296,128]{1,0:T(8,128)(2,1)S(1)}, bf16[1296,128]{1,0:T(8,128)(2,1)S(1)}, u32[]{:S(2)}, u32[]{:S(2)}) collective-permute-start(bf16[1296,128]{1,0:T(8,128)(2,1)S(1)} %collective-permute-done.7.refs_3_.refs_8_), channel_id=1, source_target_pairs={{0,1},{1,2},{2,3},{3,4},{4,5},{5,6},{6,7},{7,0},{8,9},{9,10},{10,1... | collective-permute-start | bytes 995336 | tf_op jit(solution)/shard_map/ppermute | solution.py:472
  57.9 2.4 %collective-permute-start.11 = (bf16[1296,128]{1,0:T(8,128)(2,1)S(1)}, bf16[1296,128]{1,0:T(8,128)(2,1)S(1)}, u32[]{:S(2)}, u32[]{:S(2)}) collective-permute-start(bf16[1296,128]{1,0:T(8,128)(2,1)S(1)} %collective-permute-done.8.refs_4_.refs_9_), channel_id=1, source_target_pairs={{0,7},{1,0},{2,1},{3,2},{4,3},{5,4},{6,5},{7,6},{8,15},{9,8},{10,9... | collective-permute-start | bytes 995336 | tf_op jit(solution)/shard_map/ppermute | solution.py:473
  60.3 4.6 %attend.6 = (bf16[8,2,512,256]{3,2,1,0:T(8,128)(2,1)S(1)}, f32[8,2,8,256]{3,2,1,0:T(8,128)S(1)}) custom-call(s32[8]{0:T(128)S(1)} %and_select_fusion.2.refs_0_, s32[2]{0:T(128)S(1)} %copy-done.5, bf16[8,2,640,256]{3,2,1,0:T(8,128)(2,1)S(1)} %queries.1.refs_2_, ...), custom_call_target="tpu_custom_call", output_to_operand_aliasing={{0}: (5, {}), {1}: (6, {})} | custom-call | flops 2415919104 | bytes 13631488 | tf_op jit(solution)/shard_map/attend/pallas_call | solution.py:366
  64.9 0.5 collective-permute-done.9.refs_3_.refs_10_
  65.6 3.1 %collective-permute-start.13 = (bf16[1296,128]{1,0:T(8,128)(2,1)S(1)}, bf16[1296,128]{1,0:T(8,128)(2,1)S(1)}, u32[]{:S(2)}, u32[]{:S(2)}) collective-permute-start(bf16[1296,128]{1,0:T(8,128)(2,1)S(1)} %collective-permute-done.11.refs_4_.refs_11_), channel_id=1, source_target_pairs={{0,7},{1,0},{2,1},{3,2},{4,3},{5,4},{6,5},{7,6},{8,15},{9,8},{10,9... | collective-permute-start | bytes 995336 | tf_op jit(solution)/shard_map/ppermute | solution.py:473
  68.7 4.6 %attend.7 = (bf16[8,2,512,256]{3,2,1,0:T(8,128)(2,1)S(1)}, f32[8,2,8,256]{3,2,1,0:T(8,128)S(1)}) custom-call(s32[8]{0:T(128)S(1)} %and_select_fusion.2.refs_0_, s32[2]{0:T(128)S(1)} %copy-done.5, bf16[8,2,640,256]{3,2,1,0:T(8,128)(2,1)S(1)} %queries.1.refs_2_, ...), custom_call_target="tpu_custom_call", output_to_operand_aliasing={{0}: (5, {}), {1}: (6, {})} | custom-call | flops 2415919104 | bytes 13631488 | tf_op jit(solution)/shard_map/attend/pallas_call | solution.py:366
  73.2 1.2 %collective-permute-done.10.refs_3_.refs_12_ = bf16[1296,128]{1,0:T(8,128)(2,1)S(1)} collective-permute-done((bf16[1296,128]{1,0:T(8,128)(2,1)S(1)}, bf16[1296,128]{1,0:T(8,128)(2,1)S(1)}, u32[]{:S(2)}, u32[]{:S(2)}) %collective-permute-start.10) | collective-permute-done | bytes 331808 | tf_op jit(solution)/shard_map/ppermute | solution.py:472
  74.6 3.5 %collective-permute-start.14 = (bf16[528,128]{1,0:T(8,128)(2,1)S(1)}, bf16[528,128]{1,0:T(8,128)(2,1)S(1)}, u32[]{:S(2)}, u32[]{:S(2)}) collective-permute-start(bf16[528,128]{1,0:T(8,128)(2,1)S(1)} %slice.16), channel_id=1, source_target_pairs={{0,7},{1,0},{2,1},{3,2},{4,3},{5,4},{6,5},{7,6},{8,15},{9,8},{10,9... | collective-permute-start | bytes 405512 | tf_op jit(solution)/shard_map/ppermute | solution.py:480
  78.1 4.6 %attend.8 = (bf16[8,2,512,256]{3,2,1,0:T(8,128)(2,1)S(1)}, f32[8,2,8,256]{3,2,1,0:T(8,128)S(1)}) custom-call(s32[8]{0:T(128)S(1)} %and_select_fusion.2.refs_0_, s32[2]{0:T(128)S(1)} %copy-done.5, bf16[8,2,640,256]{3,2,1,0:T(8,128)(2,1)S(1)} %queries.1.refs_2_, ...), custom_call_target="tpu_custom_call", output_to_operand_aliasing={{0}: (5, {}), {1}: (6, {})} | custom-call | flops 2415919104 | bytes 13631488 | tf_op jit(solution)/shard_map/attend/pallas_call | solution.py:366
  82.7 8.3 %attend.9 = (bf16[256,2048]{1,0:T(8,128)(2,1)}, bf16[576,256]{1,0:T(8,128)(2,1)}) custom-call(s32[8]{0:T(128)S(1)} %and_select_fusion.2.refs_0_, s32[2]{0:T(128)S(1)} %copy-done.5, bf16[8,2,640,256]{3,2,1,0:T(8,128)(2,1)S(1)} %queries.1.refs_2_, bf16[768,128]{1,0:T(8,128)(2,1)S(1)} %collective-permute-done.12.refs_3_, ...), custom_call_target="tpu_custom_call" | custom-call | flops 2415919104 | bytes 13631488 | tf_op jit(solution)/shard_map/attend/pallas_call | solution.py:366
  (40 shorter events, 0.8 us)
Async XLA Ops:
  0.6 22.6 %copy-start = (bf16[896,576]{0,1:T(8,128)(2,1)S(1)}, bf16[896,576]{0,1:T(8,128)(2,1)}, u32[]{:S(2)}) copy-start(bf16[896,576]{0,1:T(8,128)(2,1)} %param.12) | copy-start | bytes 3096580
  0.6 46.3 %copy-start.6 = (f32[512]{0:T(512)S(1)}, f32[512]{0:T(512)}, u32[]{:S(2)}) copy-start(f32[512]{0:T(512)} %param.13) | copy-start | bytes 6148
  0.7 50.5 %copy-start.3 = (bf16[256,2048]{1,0:T(8,128)(2,1)S(1)}, bf16[256,2048]{1,0:T(8,128)(2,1)}, u32[]{:S(2)}) copy-start(bf16[256,2048]{1,0:T(8,128)(2,1)} %nope_ref) | copy-start | bytes 3145732
  0.7 50.5 %copy-start.4 = (bf16[256,1024]{1,0:T(8,128)(2,1)S(1)}, bf16[256,1024]{1,0:T(8,128)(2,1)}, u32[]{:S(2)}) copy-start(bf16[256,1024]{1,0:T(8,128)(2,1)} %rope_ref.1) | copy-start | bytes 1572868
  2.6 44.6 %copy-start.7 = (s32[32]{0:T(128)S(1)}, s32[32]{0:T(128)}, u32[]{:S(2)}) copy-start(s32[32]{0:T(128)} %get-tuple-element.53.pick_ref) | copy-start | bytes 388
  2.6 13.0 %all-to-all-start = ((s32[32,1,2]{2,1,0:T(1,128)}), s32[32,1,2]{2,1,0:T(1,128)S(1)}, u32[]{:S(2)}, u32[]{:S(2)}) async-start(s32[32,1,2]{2,1,0:T(1,128)} %get-tuple-element.39), calls=%async_computation | async-start | bytes 32768 | tf_op jit(solution)/shard_map/all_to_all | solution.py:437
  17.4 29.7 %all-to-all-start.1 = ((bf16[32,2,8,576]{3,2,1,0:T(8,128)(2,1)}), bf16[32,2,8,576]{3,2,1,0:T(8,128)(2,1)S(1)}, u32[]{:S(2)}, u32[]{:S(2)}) async-start(bf16[32,2,8,576]{3,2,1,0:T(8,128)(2,1)} %gather_pages.1), calls=%async_computation.1 | async-start | bytes 1310720 | tf_op jit(solution)/shard_map/all_to_all | solution.py:443
  25.4 11.7 %collective-permute-start = (bf16[32,576]{1,0:T(8,128)(2,1)S(1)}, bf16[32,576]{1,0:T(8,128)(2,1)S(1)}, u32[]{:S(2)}, u32[]{:S(2)}) collective-permute-start(bf16[32,576]{1,0:T(8,128)(2,1)S(1)} %get-tuple-element.45), channel_id=1, source_target_pairs={{0,1},{1,0},{2,3},{3,2},{4,5},{5,4},{6,7},{7,6},{8,9},{9,8},{10,11... | collective-permute-start | bytes 110600 | tf_op jit(solution)/shard_map/ppermute | solution.py:434
  27.4 14.3 %collective-permute-start.1 = (bf16[32,576]{1,0:T(8,128)(2,1)S(1)}, bf16[32,576]{1,0:T(8,128)(2,1)S(1)}, u32[]{:S(2)}, u32[]{:S(2)}) collective-permute-start(bf16[32,576]{1,0:T(8,128)(2,1)S(1)} %get-tuple-element.46), channel_id=1, source_target_pairs={{0,2},{1,3},{2,0},{3,1},{4,6},{5,7},{6,4},{7,5},{8,10},{9,11},{10,... | collective-permute-start | bytes 110600 | tf_op jit(solution)/shard_map/ppermute | solution.py:434
  30.7 11.2 %collective-permute-start.2 = (bf16[32,576]{1,0:T(8,128)(2,1)S(1)}, bf16[32,576]{1,0:T(8,128)(2,1)S(1)}, u32[]{:S(2)}, u32[]{:S(2)}) collective-permute-start(bf16[32,576]{1,0:T(8,128)(2,1)S(1)} %get-tuple-element.47), channel_id=1, source_target_pairs={{0,3},{1,2},{2,1},{3,0},{4,7},{5,6},{6,5},{7,4},{8,11},{9,10},{10,... | collective-permute-start | bytes 110600 | tf_op jit(solution)/shard_map/ppermute | solution.py:434
  30.7 11.2 %collective-permute-start.3 = (bf16[32,576]{1,0:T(8,128)(2,1)S(1)}, bf16[32,576]{1,0:T(8,128)(2,1)S(1)}, u32[]{:S(2)}, u32[]{:S(2)}) collective-permute-start(bf16[32,576]{1,0:T(8,128)(2,1)S(1)} %get-tuple-element.48), channel_id=1, source_target_pairs={{0,4},{1,5},{2,6},{3,7},{4,0},{5,1},{6,2},{7,3},{8,12},{9,13},{10,... | collective-permute-start | bytes 110600 | tf_op jit(solution)/shard_map/ppermute | solution.py:434
  37.1 7.1 %collective-permute-start.4 = (bf16[32,576]{1,0:T(8,128)(2,1)S(1)}, bf16[32,576]{1,0:T(8,128)(2,1)S(1)}, u32[]{:S(2)}, u32[]{:S(2)}) collective-permute-start(bf16[32,576]{1,0:T(8,128)(2,1)S(1)} %get-tuple-element.49), channel_id=1, source_target_pairs={{0,5},{1,4},{2,7},{3,6},{4,1},{5,0},{6,3},{7,2},{8,13},{9,12},{10,... | collective-permute-start | bytes 110600 | tf_op jit(solution)/shard_map/ppermute | solution.py:434
  37.1 7.1 %collective-permute-start.5 = (bf16[32,576]{1,0:T(8,128)(2,1)S(1)}, bf16[32,576]{1,0:T(8,128)(2,1)S(1)}, u32[]{:S(2)}, u32[]{:S(2)}) collective-permute-start(bf16[32,576]{1,0:T(8,128)(2,1)S(1)} %get-tuple-element.50), channel_id=1, source_target_pairs={{0,6},{1,7},{2,4},{3,5},{4,2},{5,3},{6,0},{7,1},{8,14},{9,15},{10,... | collective-permute-start | bytes 110600 | tf_op jit(solution)/shard_map/ppermute | solution.py:434
  41.7 5.2 %collective-permute-start.6 = (bf16[32,576]{1,0:T(8,128)(2,1)S(1)}, bf16[32,576]{1,0:T(8,128)(2,1)S(1)}, u32[]{:S(2)}, u32[]{:S(2)}) collective-permute-start(bf16[32,576]{1,0:T(8,128)(2,1)S(1)} %get-tuple-element.51), channel_id=1, source_target_pairs={{0,7},{1,6},{2,5},{3,4},{4,3},{5,2},{6,1},{7,0},{8,15},{9,14},{10,... | collective-permute-start | bytes 110600 | tf_op jit(solution)/shard_map/ppermute | solution.py:434
  47.8 9.1 %collective-permute-start.7 = (bf16[1296,128]{1,0:T(8,128)(2,1)S(1)}, bf16[1296,128]{1,0:T(8,128)(2,1)S(1)}, u32[]{:S(2)}, u32[]{:S(2)}) collective-permute-start(bf16[1296,128]{1,0:T(8,128)(2,1)S(1)} %select_pages.1.refs_3_.refs_7_), channel_id=1, source_target_pairs={{0,1},{1,2},{2,3},{3,4},{4,5},{5,6},{6,7},{7,0},{8,9},{9,10},{10,1... | collective-permute-start | bytes 995336 | tf_op jit(solution)/shard_map/ppermute | solution.py:466
  49.8 7.2 %collective-permute-start.8 = (bf16[1296,128]{1,0:T(8,128)(2,1)S(1)}, bf16[1296,128]{1,0:T(8,128)(2,1)S(1)}, u32[]{:S(2)}, u32[]{:S(2)}) collective-permute-start(bf16[1296,128]{1,0:T(8,128)(2,1)S(1)} %select_pages.1.refs_3_.refs_7_), channel_id=1, source_target_pairs={{0,7},{1,0},{2,1},{3,2},{4,3},{5,4},{6,5},{7,6},{8,15},{9,8},{10,9... | collective-permute-start | bytes 995336 | tf_op jit(solution)/shard_map/ppermute | solution.py:466
  51.1 1.6 %copy-start.1 = (bf16[16,128,512]{2,1,0:T(8,128)(2,1)S(1)}, bf16[16,128,512]{2,1,0:T(8,128)(2,1)}, u32[]{:S(2)}) copy-start(bf16[16,128,512]{2,1,0:T(8,128)(2,1)} %absorb_ref.1) | copy-start | bytes 6291460
  52.7 1.3 %copy-start.5 = (s32[2]{0:T(128)S(1)}, s32[2]{0:T(128)}, u32[]{:S(2)}) copy-start(s32[2]{0:T(128)} %refs_1_.9) | copy-start | bytes 28
  57.0 8.4 %collective-permute-start.9 = (bf16[1296,128]{1,0:T(8,128)(2,1)S(1)}, bf16[1296,128]{1,0:T(8,128)(2,1)S(1)}, u32[]{:S(2)}, u32[]{:S(2)}) collective-permute-start(bf16[1296,128]{1,0:T(8,128)(2,1)S(1)} %collective-permute-done.7.refs_3_.refs_8_), channel_id=1, source_target_pairs={{0,1},{1,2},{2,3},{3,4},{4,5},{5,6},{6,7},{7,0},{8,9},{9,10},{10,1... | collective-permute-start | bytes 995336 | tf_op jit(solution)/shard_map/ppermute | solution.py:472
  57.9 7.6 %collective-permute-start.11 = (bf16[1296,128]{1,0:T(8,128)(2,1)S(1)}, bf16[1296,128]{1,0:T(8,128)(2,1)S(1)}, u32[]{:S(2)}, u32[]{:S(2)}) collective-permute-start(bf16[1296,128]{1,0:T(8,128)(2,1)S(1)} %collective-permute-done.8.refs_4_.refs_9_), channel_id=1, source_target_pairs={{0,7},{1,0},{2,1},{3,2},{4,3},{5,4},{6,5},{7,6},{8,15},{9,8},{10,9... | collective-permute-start | bytes 995336 | tf_op jit(solution)/shard_map/ppermute | solution.py:473
  65.4 9.0 %collective-permute-start.10 = (bf16[1296,128]{1,0:T(8,128)(2,1)S(1)}, bf16[1296,128]{1,0:T(8,128)(2,1)S(1)}, u32[]{:S(2)}, u32[]{:S(2)}) collective-permute-start(bf16[1296,128]{1,0:T(8,128)(2,1)S(1)} %collective-permute-done.9.refs_3_.refs_10_), channel_id=1, source_target_pairs={{0,1},{1,2},{2,3},{3,4},{4,5},{5,6},{6,7},{7,0},{8,9},{9,10},{10,1... | collective-permute-start | bytes 995336 | tf_op jit(solution)/shard_map/ppermute | solution.py:472
  65.6 9.0 %collective-permute-start.13 = (bf16[1296,128]{1,0:T(8,128)(2,1)S(1)}, bf16[1296,128]{1,0:T(8,128)(2,1)S(1)}, u32[]{:S(2)}, u32[]{:S(2)}) collective-permute-start(bf16[1296,128]{1,0:T(8,128)(2,1)S(1)} %collective-permute-done.11.refs_4_.refs_11_), channel_id=1, source_target_pairs={{0,7},{1,0},{2,1},{3,2},{4,3},{5,4},{6,5},{7,6},{8,15},{9,8},{10,9... | collective-permute-start | bytes 995336 | tf_op jit(solution)/shard_map/ppermute | solution.py:473
  74.4 8.2 %collective-permute-start.12 = (bf16[768,128]{1,0:T(8,128)(2,1)S(1)}, bf16[768,128]{1,0:T(8,128)(2,1)S(1)}, u32[]{:S(2)}, u32[]{:S(2)}) collective-permute-start(bf16[768,128]{1,0:T(8,128)(2,1)S(1)} %slice.14), channel_id=1, source_target_pairs={{0,1},{1,2},{2,3},{3,4},{4,5},{5,6},{6,7},{7,0},{8,9},{9,10},{10,1... | collective-permute-start | bytes 589832 | tf_op jit(solution)/shard_map/ppermute | solution.py:480
  74.6 8.1 %copy-start.2 = (bf16[16,512,128]{2,1,0:T(8,128)(2,1)S(1)}, bf16[16,512,128]{2,1,0:T(8,128)(2,1)}, u32[]{:S(2)}) copy-start(bf16[16,512,128]{2,1,0:T(8,128)(2,1)} %refs_14_.1) | copy-start | bytes 6291460
  74.6 8.1 %collective-permute-start.14 = (bf16[528,128]{1,0:T(8,128)(2,1)S(1)}, bf16[528,128]{1,0:T(8,128)(2,1)S(1)}, u32[]{:S(2)}, u32[]{:S(2)}) collective-permute-start(bf16[528,128]{1,0:T(8,128)(2,1)S(1)} %slice.16), channel_id=1, source_target_pairs={{0,7},{1,0},{2,1},{3,2},{4,3},{5,4},{6,5},{7,6},{8,15},{9,8},{10,9... | collective-permute-start | bytes 405512 | tf_op jit(solution)/shard_map/ppermute | solution.py:480

commit v4 on v3

--- a/solution.py
+++ b/solution.py
@@ -423,7 +423,8 @@
     split = page // tp_size
     cols = kv_rank // LANES
 
-    place = jnp.stack([z ^ i for i in range(tp_size)]).astype(jnp.int32)
+    others = sorted(range(1, tp_size), key=lambda i: -min(i, tp_size - i))
+    place = jnp.stack([z] + [z ^ i for i in others]).astype(jnp.int32)
     origins = ((z + jnp.arange(tp_size, dtype=jnp.int32)) % tp_size).astype(jnp.int32)
     own_rows = rows // tp_size
     token = z * own_rows + jnp.arange(own_rows, dtype=jnp.int32)
@@ -446,7 +447,7 @@
     gain = latent_gain[None, :]
     part = jnp.dot(hidden_in, kv_down, preferred_element_type=F32)
     kept, *gives = deal(place, part, tp_size)
-    got = [swap(given, i + 1) for i, given in enumerate(gives)]
+    got = [swap(given, i) for i, given in zip(others, gives)]
     fresh = finish_latents(kept, gain, cosine, sine, got)
     fetched, fresh, q_nope = lax.optimization_barrier((fetched, fresh, q_nope))
 

time: 91.3 us -> 92.5 us (1.013)
  waiting for transfers between devices: 8.59 us -> 9.56 us
    ppermute x2, waiting for transfers between devices: 1.7 us -> 2.65 us  [shards(): next_right = lax.ppermute(right, 'tp', up)]
  transfers between devices with their start and end apart: 17 -> 17, of which waited for: 6 -> 8; matrix products, arithmetic and copies ran while one was open for 6% -> 6% of each run, Pallas kernels for 21% -> 20%
where the time goes in v4:
time: 92.5 us; the launch traced here: 92.1 us
  starting transfers between devices  43.2 us (47%)
  Pallas kernels  31.3 us (34%)
  waiting for transfers between devices  9.56 us (10%)
  local copies, waits for them, and re-layouts  4.13 us (4%)
  matrix products  1.6 us (2%)
  other arithmetic  1.42 us (2%)
    pallas_call x5, Pallas kernels, attend(): pl.pallas_call(functools.partial(attend_body, pieces=tuple((len(parts) fo...  24.9 us
    ppermute x7, starting transfers between devices, swap(): return lax.ppermute(given, 'tp', [(i, i ^ far) for i in range(tp_size)])  16.3 us
    all_to_all x1, starting transfers between devices, shards(): asked = lax.all_to_all(want, 'dp', split_axis=0, concat_axis=0, tiled=True)  7.62 us
    all_to_all x1, starting transfers between devices, shards(): lax.all_to_all(reply, 'dp', split_axis=0, concat_axis=0, tiled=True)  5.8 us
    ppermute x2, starting transfers between devices, shards(): next_left = lax.ppermute(left, 'tp', down)  5.47 us
    ppermute x7, waiting for transfers between devices, swap(): return lax.ppermute(given, 'tp', [(i, i ^ far) for i in range(tp_size)])  5.07 us
    ppermute x1, starting transfers between devices, shards(): lax.ppermute(left[cut:], 'tp', down)  3.52 us
    ppermute x2, starting transfers between devices, shards(): right, left = (lax.ppermute(own, 'tp', up), lax.ppermute(own, 'tp', down))  3.31 us
  transfers between devices with their start and end apart: 17, of which 8 were waited for; matrix products, arithmetic and copies ran while one was open for 6% of the time, Pallas kernels for 20%

profile of v4, /device:TPU:6, one launch (start us, length us, event | category | flops | bytes accessed | tf_op | source)
XLA Modules:
  0.0 92.1 jit_solution(3913483784848220564)
XLA Ops:
  0.7 1.9 %plan.1 = (s32[32,1,2]{2,1,0:T(1,128)}, s32[32]{0:T(128)}) custom-call(s32[2,16]{1,0:T(2,128)} %bitcast.18, s32[2,16]{1,0:T(2,128)} %slot_ref.1), custom_call_target="tpu_custom_call" | custom-call | tf_op jit(solution)/shard_map/plan/pallas_call | solution.py:99
  2.6 7.6 %all-to-all-start = ((s32[32,1,2]{2,1,0:T(1,128)}), s32[32,1,2]{2,1,0:T(1,128)S(1)}, u32[]{:S(2)}, u32[]{:S(2)}) async-start(s32[32,1,2]{2,1,0:T(1,128)} %get-tuple-element.39), calls=%async_computation | async-start | bytes 32768 | tf_op jit(solution)/shard_map/all_to_all | solution.py:438
  10.3 1.3 %fusion.2 = (s32[1]{0:T(128)}, s32[1]{0:T(128)}) fusion(s32[2]{0:T(128)} %refs_1_.9), kind=kLoop, calls=%fused_computation.15 | loop fusion | bytes 16 | tf_op jit(solution)/shard_map/slice | solution.py:431
  11.6 1.1 %constant_dynamic-slice_fusion.pages_ref = bf16[48,8,576]{2,1,0:T(8,128)(2,1)S(1)} fusion(bf16[48,64,576]{2,1,0:T(8,128)(2,1)} %param.18, s32[]{:T(128)S(6)} %select_n.26), kind=kLoop, calls=%fused_computation.14 | loop fusion | bytes 884740 | tf_op jit(solution)/shard_map/dynamic_slice | solution.py:432
  12.7 1.3 %fusion = s32[32]{0:T(128)S(1)} fusion(s32[]{:T(128)} %bitcast.10, s32[]{:T(128)} %bitcast.9, s32[]{:T(128)S(6)} %mul.20), kind=kLoop, calls=%fused_computation.11 | loop fusion | flops 736 | bytes 140 | tf_op jit(solution)/shard_map/add | solution.py:431
  14.0 1.6 %all-to-all-done.ids_ref = s32[32,1,2]{2,1,0:T(1,128)S(1)} async-done(((s32[32,1,2]{2,1,0:T(1,128)}), s32[32,1,2]{2,1,0:T(1,128)S(1)}, u32[]{:S(2)}, u32[]{:S(2)}) %all-to-all-start) | async-done | bytes 288 | tf_op jit(solution)/shard_map/all_to_all | solution.py:438
  15.6 1.8 %gather_pages.1 = bf16[32,2,8,576]{3,2,1,0:T(8,128)(2,1)} custom-call(s32[32,1,2]{2,1,0:T(1,128)S(1)} %all-to-all-done.ids_ref, bf16[48,8,576]{2,1,0:T(8,128)(2,1)S(1)} %constant_dynamic-slice_fusion.pages_ref), custom_call_target="tpu_custom_call" | custom-call | tf_op jit(solution)/shard_map/gather_pages/pallas_call | solution.py:119
  17.4 5.8 %all-to-all-start.1 = ((bf16[32,2,8,576]{3,2,1,0:T(8,128)(2,1)}), bf16[32,2,8,576]{3,2,1,0:T(8,128)(2,1)S(1)}, u32[]{:S(2)}, u32[]{:S(2)}) async-start(bf16[32,2,8,576]{3,2,1,0:T(8,128)(2,1)} %gather_pages.1), calls=%async_computation.1 | async-start | bytes 1310720 | tf_op jit(solution)/shard_map/all_to_all | solution.py:444
  23.2 1.6 %fusion.3.part_ref = f32[256,576]{1,0:T(8,128)S(1)} fusion(bf16[256,896]{1,0:T(8,128)(2,1)} %param.11, bf16[896,576]{0,1:T(8,128)(2,1)S(1)} %copy-done), kind=kOutput, calls=%fused_computation.16 | convolution fusion | flops 264241152 | bytes 2080768 | tf_op jit(solution)/shard_map/dot_general | solution.py:448
  25.4 7.3 %collective-permute-start = (bf16[32,576]{1,0:T(8,128)(2,1)S(1)}, bf16[32,576]{1,0:T(8,128)(2,1)S(1)}, u32[]{:S(2)}, u32[]{:S(2)}) collective-permute-start(bf16[32,576]{1,0:T(8,128)(2,1)S(1)} %get-tuple-element.45), channel_id=1, source_target_pairs={{0,4},{1,5},{2,6},{3,7},{4,0},{5,1},{6,2},{7,3},{8,12},{9,13},{10,... | collective-permute-start | bytes 110600 | tf_op jit(solution)/shard_map/ppermute | solution.py:435
  32.7 1.9 %collective-permute-start.1 = (bf16[32,576]{1,0:T(8,128)(2,1)S(1)}, bf16[32,576]{1,0:T(8,128)(2,1)S(1)}, u32[]{:S(2)}, u32[]{:S(2)}) collective-permute-start(bf16[32,576]{1,0:T(8,128)(2,1)S(1)} %get-tuple-element.46), channel_id=1, source_target_pairs={{0,3},{1,2},{2,1},{3,0},{4,7},{5,6},{6,5},{7,4},{8,11},{9,10},{10,... | collective-permute-start | bytes 110600 | tf_op jit(solution)/shard_map/ppermute | solution.py:435
  34.7 1.1 %collective-permute-start.3 = (bf16[32,576]{1,0:T(8,128)(2,1)S(1)}, bf16[32,576]{1,0:T(8,128)(2,1)S(1)}, u32[]{:S(2)}, u32[]{:S(2)}) collective-permute-start(bf16[32,576]{1,0:T(8,128)(2,1)S(1)} %get-tuple-element.48), channel_id=1, source_target_pairs={{0,2},{1,3},{2,0},{3,1},{4,6},{5,7},{6,4},{7,5},{8,10},{9,11},{10,... | collective-permute-start | bytes 110600 | tf_op jit(solution)/shard_map/ppermute | solution.py:435
  35.8 4.0 %collective-permute-start.4 = (bf16[32,576]{1,0:T(8,128)(2,1)S(1)}, bf16[32,576]{1,0:T(8,128)(2,1)S(1)}, u32[]{:S(2)}, u32[]{:S(2)}) collective-permute-start(bf16[32,576]{1,0:T(8,128)(2,1)S(1)} %get-tuple-element.49), channel_id=1, source_target_pairs={{0,6},{1,7},{2,4},{3,5},{4,2},{5,3},{6,0},{7,1},{8,14},{9,15},{10,... | collective-permute-start | bytes 110600 | tf_op jit(solution)/shard_map/ppermute | solution.py:435
  39.8 1.9 %collective-permute-start.5 = (bf16[32,576]{1,0:T(8,128)(2,1)S(1)}, bf16[32,576]{1,0:T(8,128)(2,1)S(1)}, u32[]{:S(2)}, u32[]{:S(2)}) collective-permute-start(bf16[32,576]{1,0:T(8,128)(2,1)S(1)} %get-tuple-element.50), channel_id=1, source_target_pairs={{0,1},{1,0},{2,3},{3,2},{4,5},{5,4},{6,7},{7,6},{8,9},{9,8},{10,11... | collective-permute-start | bytes 110600 | tf_op jit(solution)/shard_map/ppermute | solution.py:435
  42.2 0.9 collective-permute-done.4.rest_4_
  43.1 1.0 %collective-permute-done.5.rest_5_ = bf16[32,576]{1,0:T(8,128)(2,1)S(1)} collective-permute-done((bf16[32,576]{1,0:T(8,128)(2,1)S(1)}, bf16[32,576]{1,0:T(8,128)(2,1)S(1)}, u32[]{:S(2)}, u32[]{:S(2)}) %collective-permute-start.5) | collective-permute-done | bytes 36896 | tf_op jit(solution)/shard_map/ppermute | solution.py:435
  44.1 2.8 %collective-permute-done.6.rest_6_ = bf16[32,576]{1,0:T(8,128)(2,1)S(1)} collective-permute-done((bf16[32,576]{1,0:T(8,128)(2,1)S(1)}, bf16[32,576]{1,0:T(8,128)(2,1)S(1)}, u32[]{:S(2)}, u32[]{:S(2)}) %collective-permute-start.6) | collective-permute-done | bytes 36896 | tf_op jit(solution)/shard_map/ppermute | solution.py:435
  47.8 2.0 %collective-permute-start.7 = (bf16[1296,128]{1,0:T(8,128)(2,1)S(1)}, bf16[1296,128]{1,0:T(8,128)(2,1)S(1)}, u32[]{:S(2)}, u32[]{:S(2)}) collective-permute-start(bf16[1296,128]{1,0:T(8,128)(2,1)S(1)} %select_pages.1.refs_3_.refs_7_), channel_id=1, source_target_pairs={{0,1},{1,2},{2,3},{3,4},{4,5},{5,6},{6,7},{7,0},{8,9},{9,10},{10,1... | collective-permute-start | bytes 995336 | tf_op jit(solution)/shard_map/ppermute | solution.py:467
  49.8 1.3 %collective-permute-start.8 = (bf16[1296,128]{1,0:T(8,128)(2,1)S(1)}, bf16[1296,128]{1,0:T(8,128)(2,1)S(1)}, u32[]{:S(2)}, u32[]{:S(2)}) collective-permute-start(bf16[1296,128]{1,0:T(8,128)(2,1)S(1)} %select_pages.1.refs_3_.refs_7_), channel_id=1, source_target_pairs={{0,7},{1,0},{2,1},{3,2},{4,3},{5,4},{6,5},{7,6},{8,15},{9,8},{10,9... | collective-permute-start | bytes 995336 | tf_op jit(solution)/shard_map/ppermute | solution.py:467
  51.2 1.6 %copy-done.1 = bf16[16,128,512]{2,1,0:T(8,128)(2,1)S(1)} copy-done((bf16[16,128,512]{2,1,0:T(8,128)(2,1)S(1)}, bf16[16,128,512]{2,1,0:T(8,128)(2,1)}, u32[]{:S(2)}) %copy-start.1) | copy-done | bytes 2097176
  52.7 1.3 %queries.1.refs_2_ = bf16[8,2,640,256]{3,2,1,0:T(8,128)(2,1)S(1)} custom-call(bf16[256,2048]{1,0:T(8,128)(2,1)S(1)} %copy-done.3, bf16[256,1024]{1,0:T(8,128)(2,1)S(1)} %copy-done.4, bf16[16,128,512]{2,1,0:T(8,128)(2,1)S(1)} %copy-done.1), custom_call_target="tpu_custom_call" | custom-call | tf_op jit(solution)/shard_map/queries/pallas_call | solution.py:201
  54.1 2.9 %attend.5 = (bf16[8,2,512,256]{3,2,1,0:T(8,128)(2,1)S(1)}, f32[8,2,8,256]{3,2,1,0:T(8,128)S(1)}) custom-call(s32[8]{0:T(128)S(1)} %and_select_fusion.2.refs_0_, s32[2]{0:T(128)S(1)} %copy-done.5, bf16[8,2,640,256]{3,2,1,0:T(8,128)(2,1)S(1)} %queries.1.refs_2_, bf16[1296,128]{1,0:T(8,128)(2,1)S(1)} %select_pages.1.refs_3_.refs_7_), custom_call_target="tpu_custom_call" | custom-call | flops 1207959552 | bytes 13631488 | tf_op jit(solution)/shard_map/attend/pallas_call | solution.py:366
  57.0 0.9 %collective-permute-start.9 = (bf16[1296,128]{1,0:T(8,128)(2,1)S(1)}, bf16[1296,128]{1,0:T(8,128)(2,1)S(1)}, u32[]{:S(2)}, u32[]{:S(2)}) collective-permute-start(bf16[1296,128]{1,0:T(8,128)(2,1)S(1)} %collective-permute-done.7.refs_3_.refs_8_), channel_id=1, source_target_pairs={{0,1},{1,2},{2,3},{3,4},{4,5},{5,6},{6,7},{7,0},{8,9},{9,10},{10,1... | collective-permute-start | bytes 995336 | tf_op jit(solution)/shard_map/ppermute | solution.py:473
  57.9 2.4 %collective-permute-start.11 = (bf16[1296,128]{1,0:T(8,128)(2,1)S(1)}, bf16[1296,128]{1,0:T(8,128)(2,1)S(1)}, u32[]{:S(2)}, u32[]{:S(2)}) collective-permute-start(bf16[1296,128]{1,0:T(8,128)(2,1)S(1)} %collective-permute-done.8.refs_4_.refs_9_), channel_id=1, source_target_pairs={{0,7},{1,0},{2,1},{3,2},{4,3},{5,4},{6,5},{7,6},{8,15},{9,8},{10,9... | collective-permute-start | bytes 995336 | tf_op jit(solution)/shard_map/ppermute | solution.py:474
  60.3 4.6 %attend.6 = (bf16[8,2,512,256]{3,2,1,0:T(8,128)(2,1)S(1)}, f32[8,2,8,256]{3,2,1,0:T(8,128)S(1)}) custom-call(s32[8]{0:T(128)S(1)} %and_select_fusion.2.refs_0_, s32[2]{0:T(128)S(1)} %copy-done.5, bf16[8,2,640,256]{3,2,1,0:T(8,128)(2,1)S(1)} %queries.1.refs_2_, ...), custom_call_target="tpu_custom_call", output_to_operand_aliasing={{0}: (5, {}), {1}: (6, {})} | custom-call | flops 2415919104 | bytes 13631488 | tf_op jit(solution)/shard_map/attend/pallas_call | solution.py:366
  64.9 0.9 collective-permute-done.9.refs_3_.refs_10_
  66.1 3.1 %collective-permute-start.13 = (bf16[1296,128]{1,0:T(8,128)(2,1)S(1)}, bf16[1296,128]{1,0:T(8,128)(2,1)S(1)}, u32[]{:S(2)}, u32[]{:S(2)}) collective-permute-start(bf16[1296,128]{1,0:T(8,128)(2,1)S(1)} %collective-permute-done.11.refs_4_.refs_11_), channel_id=1, source_target_pairs={{0,7},{1,0},{2,1},{3,2},{4,3},{5,4},{6,5},{7,6},{8,15},{9,8},{10,9... | collective-permute-start | bytes 995336 | tf_op jit(solution)/shard_map/ppermute | solution.py:474
  69.2 4.6 %attend.7 = (bf16[8,2,512,256]{3,2,1,0:T(8,128)(2,1)S(1)}, f32[8,2,8,256]{3,2,1,0:T(8,128)S(1)}) custom-call(s32[8]{0:T(128)S(1)} %and_select_fusion.2.refs_0_, s32[2]{0:T(128)S(1)} %copy-done.5, bf16[8,2,640,256]{3,2,1,0:T(8,128)(2,1)S(1)} %queries.1.refs_2_, ...), custom_call_target="tpu_custom_call", output_to_operand_aliasing={{0}: (5, {}), {1}: (6, {})} | custom-call | flops 2415919104 | bytes 13631488 | tf_op jit(solution)/shard_map/attend/pallas_call | solution.py:366
  73.8 1.8 %collective-permute-done.10.refs_3_.refs_12_ = bf16[1296,128]{1,0:T(8,128)(2,1)S(1)} collective-permute-done((bf16[1296,128]{1,0:T(8,128)(2,1)S(1)}, bf16[1296,128]{1,0:T(8,128)(2,1)S(1)}, u32[]{:S(2)}, u32[]{:S(2)}) %collective-permute-start.10) | collective-permute-done | bytes 331808 | tf_op jit(solution)/shard_map/ppermute | solution.py:473
  75.8 3.5 %collective-permute-start.14 = (bf16[528,128]{1,0:T(8,128)(2,1)S(1)}, bf16[528,128]{1,0:T(8,128)(2,1)S(1)}, u32[]{:S(2)}, u32[]{:S(2)}) collective-permute-start(bf16[528,128]{1,0:T(8,128)(2,1)S(1)} %slice.16), channel_id=1, source_target_pairs={{0,7},{1,0},{2,1},{3,2},{4,3},{5,4},{6,5},{7,6},{8,15},{9,8},{10,9... | collective-permute-start | bytes 405512 | tf_op jit(solution)/shard_map/ppermute | solution.py:481
  79.3 4.6 %attend.8 = (bf16[8,2,512,256]{3,2,1,0:T(8,128)(2,1)S(1)}, f32[8,2,8,256]{3,2,1,0:T(8,128)S(1)}) custom-call(s32[8]{0:T(128)S(1)} %and_select_fusion.2.refs_0_, s32[2]{0:T(128)S(1)} %copy-done.5, bf16[8,2,640,256]{3,2,1,0:T(8,128)(2,1)S(1)} %queries.1.refs_2_, ...), custom_call_target="tpu_custom_call", output_to_operand_aliasing={{0}: (5, {}), {1}: (6, {})} | custom-call | flops 2415919104 | bytes 13631488 | tf_op jit(solution)/shard_map/attend/pallas_call | solution.py:366
  83.9 8.3 %attend.9 = (bf16[256,2048]{1,0:T(8,128)(2,1)}, bf16[576,256]{1,0:T(8,128)(2,1)}) custom-call(s32[8]{0:T(128)S(1)} %and_select_fusion.2.refs_0_, s32[2]{0:T(128)S(1)} %copy-done.5, bf16[8,2,640,256]{3,2,1,0:T(8,128)(2,1)S(1)} %queries.1.refs_2_, bf16[768,128]{1,0:T(8,128)(2,1)S(1)} %collective-permute-done.12.refs_3_, ...), custom_call_target="tpu_custom_call" | custom-call | flops 2415919104 | bytes 13631488 | tf_op jit(solution)/shard_map/attend/pallas_call | solution.py:366
  (40 shorter events, 2.6 us)
Async XLA Ops:
  0.6 22.6 %copy-start = (bf16[896,576]{0,1:T(8,128)(2,1)S(1)}, bf16[896,576]{0,1:T(8,128)(2,1)}, u32[]{:S(2)}) copy-start(bf16[896,576]{0,1:T(8,128)(2,1)} %param.12) | copy-start | bytes 3096580
  0.6 46.3 %copy-start.6 = (f32[512]{0:T(512)S(1)}, f32[512]{0:T(512)}, u32[]{:S(2)}) copy-start(f32[512]{0:T(512)} %param.13) | copy-start | bytes 6148
  0.7 50.5 %copy-start.3 = (bf16[256,2048]{1,0:T(8,128)(2,1)S(1)}, bf16[256,2048]{1,0:T(8,128)(2,1)}, u32[]{:S(2)}) copy-start(bf16[256,2048]{1,0:T(8,128)(2,1)} %nope_ref) | copy-start | bytes 3145732
  0.7 50.5 %copy-start.4 = (bf16[256,1024]{1,0:T(8,128)(2,1)S(1)}, bf16[256,1024]{1,0:T(8,128)(2,1)}, u32[]{:S(2)}) copy-start(bf16[256,1024]{1,0:T(8,128)(2,1)} %rope_ref.1) | copy-start | bytes 1572868
  2.6 44.6 %copy-start.7 = (s32[32]{0:T(128)S(1)}, s32[32]{0:T(128)}, u32[]{:S(2)}) copy-start(s32[32]{0:T(128)} %get-tuple-element.53.pick_ref) | copy-start | bytes 388
  2.6 13.0 %all-to-all-start = ((s32[32,1,2]{2,1,0:T(1,128)}), s32[32,1,2]{2,1,0:T(1,128)S(1)}, u32[]{:S(2)}, u32[]{:S(2)}) async-start(s32[32,1,2]{2,1,0:T(1,128)} %get-tuple-element.39), calls=%async_computation | async-start | bytes 32768 | tf_op jit(solution)/shard_map/all_to_all | solution.py:438
  17.4 29.7 %all-to-all-start.1 = ((bf16[32,2,8,576]{3,2,1,0:T(8,128)(2,1)}), bf16[32,2,8,576]{3,2,1,0:T(8,128)(2,1)S(1)}, u32[]{:S(2)}, u32[]{:S(2)}) async-start(bf16[32,2,8,576]{3,2,1,0:T(8,128)(2,1)} %gather_pages.1), calls=%async_computation.1 | async-start | bytes 1310720 | tf_op jit(solution)/shard_map/all_to_all | solution.py:444
  25.4 14.4 %collective-permute-start = (bf16[32,576]{1,0:T(8,128)(2,1)S(1)}, bf16[32,576]{1,0:T(8,128)(2,1)S(1)}, u32[]{:S(2)}, u32[]{:S(2)}) collective-permute-start(bf16[32,576]{1,0:T(8,128)(2,1)S(1)} %get-tuple-element.45), channel_id=1, source_target_pairs={{0,4},{1,5},{2,6},{3,7},{4,0},{5,1},{6,2},{7,3},{8,12},{9,13},{10,... | collective-permute-start | bytes 110600 | tf_op jit(solution)/shard_map/ppermute | solution.py:435
  32.7 9.0 %collective-permute-start.1 = (bf16[32,576]{1,0:T(8,128)(2,1)S(1)}, bf16[32,576]{1,0:T(8,128)(2,1)S(1)}, u32[]{:S(2)}, u32[]{:S(2)}) collective-permute-start(bf16[32,576]{1,0:T(8,128)(2,1)S(1)} %get-tuple-element.46), channel_id=1, source_target_pairs={{0,3},{1,2},{2,1},{3,0},{4,7},{5,6},{6,5},{7,4},{8,11},{9,10},{10,... | collective-permute-start | bytes 110600 | tf_op jit(solution)/shard_map/ppermute | solution.py:435
  34.7 7.6 %collective-permute-start.2 = (bf16[32,576]{1,0:T(8,128)(2,1)S(1)}, bf16[32,576]{1,0:T(8,128)(2,1)S(1)}, u32[]{:S(2)}, u32[]{:S(2)}) collective-permute-start(bf16[32,576]{1,0:T(8,128)(2,1)S(1)} %get-tuple-element.47), channel_id=1, source_target_pairs={{0,5},{1,4},{2,7},{3,6},{4,1},{5,0},{6,3},{7,2},{8,13},{9,12},{10,... | collective-permute-start | bytes 110600 | tf_op jit(solution)/shard_map/ppermute | solution.py:435
  34.7 7.6 %collective-permute-start.3 = (bf16[32,576]{1,0:T(8,128)(2,1)S(1)}, bf16[32,576]{1,0:T(8,128)(2,1)S(1)}, u32[]{:S(2)}, u32[]{:S(2)}) collective-permute-start(bf16[32,576]{1,0:T(8,128)(2,1)S(1)} %get-tuple-element.48), channel_id=1, source_target_pairs={{0,2},{1,3},{2,0},{3,1},{4,6},{5,7},{6,4},{7,5},{8,10},{9,11},{10,... | collective-permute-start | bytes 110600 | tf_op jit(solution)/shard_map/ppermute | solution.py:435
  35.8 7.4 %collective-permute-start.4 = (bf16[32,576]{1,0:T(8,128)(2,1)S(1)}, bf16[32,576]{1,0:T(8,128)(2,1)S(1)}, u32[]{:S(2)}, u32[]{:S(2)}) collective-permute-start(bf16[32,576]{1,0:T(8,128)(2,1)S(1)} %get-tuple-element.49), channel_id=1, source_target_pairs={{0,6},{1,7},{2,4},{3,5},{4,2},{5,3},{6,0},{7,1},{8,14},{9,15},{10,... | collective-permute-start | bytes 110600 | tf_op jit(solution)/shard_map/ppermute | solution.py:435
  39.8 4.3 %collective-permute-start.5 = (bf16[32,576]{1,0:T(8,128)(2,1)S(1)}, bf16[32,576]{1,0:T(8,128)(2,1)S(1)}, u32[]{:S(2)}, u32[]{:S(2)}) collective-permute-start(bf16[32,576]{1,0:T(8,128)(2,1)S(1)} %get-tuple-element.50), channel_id=1, source_target_pairs={{0,1},{1,0},{2,3},{3,2},{4,5},{5,4},{6,7},{7,6},{8,9},{9,8},{10,11... | collective-permute-start | bytes 110600 | tf_op jit(solution)/shard_map/ppermute | solution.py:435
  41.7 5.2 %collective-permute-start.6 = (bf16[32,576]{1,0:T(8,128)(2,1)S(1)}, bf16[32,576]{1,0:T(8,128)(2,1)S(1)}, u32[]{:S(2)}, u32[]{:S(2)}) collective-permute-start(bf16[32,576]{1,0:T(8,128)(2,1)S(1)} %get-tuple-element.51), channel_id=1, source_target_pairs={{0,7},{1,6},{2,5},{3,4},{4,3},{5,2},{6,1},{7,0},{8,15},{9,14},{10,... | collective-permute-start | bytes 110600 | tf_op jit(solution)/shard_map/ppermute | solution.py:435
  47.8 9.1 %collective-permute-start.7 = (bf16[1296,128]{1,0:T(8,128)(2,1)S(1)}, bf16[1296,128]{1,0:T(8,128)(2,1)S(1)}, u32[]{:S(2)}, u32[]{:S(2)}) collective-permute-start(bf16[1296,128]{1,0:T(8,128)(2,1)S(1)} %select_pages.1.refs_3_.refs_7_), channel_id=1, source_target_pairs={{0,1},{1,2},{2,3},{3,4},{4,5},{5,6},{6,7},{7,0},{8,9},{9,10},{10,1... | collective-permute-start | bytes 995336 | tf_op jit(solution)/shard_map/ppermute | solution.py:467
  49.8 7.2 %collective-permute-start.8 = (bf16[1296,128]{1,0:T(8,128)(2,1)S(1)}, bf16[1296,128]{1,0:T(8,128)(2,1)S(1)}, u32[]{:S(2)}, u32[]{:S(2)}) collective-permute-start(bf16[1296,128]{1,0:T(8,128)(2,1)S(1)} %select_pages.1.refs_3_.refs_7_), channel_id=1, source_target_pairs={{0,7},{1,0},{2,1},{3,2},{4,3},{5,4},{6,5},{7,6},{8,15},{9,8},{10,9... | collective-permute-start | bytes 995336 | tf_op jit(solution)/shard_map/ppermute | solution.py:467
  51.1 1.6 %copy-start.1 = (bf16[16,128,512]{2,1,0:T(8,128)(2,1)S(1)}, bf16[16,128,512]{2,1,0:T(8,128)(2,1)}, u32[]{:S(2)}) copy-start(bf16[16,128,512]{2,1,0:T(8,128)(2,1)} %absorb_ref.1) | copy-start | bytes 6291460
  52.7 1.3 %copy-start.5 = (s32[2]{0:T(128)S(1)}, s32[2]{0:T(128)}, u32[]{:S(2)}) copy-start(s32[2]{0:T(128)} %refs_1_.9) | copy-start | bytes 28
  57.0 8.8 %collective-permute-start.9 = (bf16[1296,128]{1,0:T(8,128)(2,1)S(1)}, bf16[1296,128]{1,0:T(8,128)(2,1)S(1)}, u32[]{:S(2)}, u32[]{:S(2)}) collective-permute-start(bf16[1296,128]{1,0:T(8,128)(2,1)S(1)} %collective-permute-done.7.refs_3_.refs_8_), channel_id=1, source_target_pairs={{0,1},{1,2},{2,3},{3,4},{4,5},{5,6},{6,7},{7,0},{8,9},{9,10},{10,1... | collective-permute-start | bytes 995336 | tf_op jit(solution)/shard_map/ppermute | solution.py:473
  57.9 8.2 %collective-permute-start.11 = (bf16[1296,128]{1,0:T(8,128)(2,1)S(1)}, bf16[1296,128]{1,0:T(8,128)(2,1)S(1)}, u32[]{:S(2)}, u32[]{:S(2)}) collective-permute-start(bf16[1296,128]{1,0:T(8,128)(2,1)S(1)} %collective-permute-done.8.refs_4_.refs_9_), channel_id=1, source_target_pairs={{0,7},{1,0},{2,1},{3,2},{4,3},{5,4},{6,5},{7,6},{8,15},{9,8},{10,9... | collective-permute-start | bytes 995336 | tf_op jit(solution)/shard_map/ppermute | solution.py:474
  65.7 9.9 %collective-permute-start.10 = (bf16[1296,128]{1,0:T(8,128)(2,1)S(1)}, bf16[1296,128]{1,0:T(8,128)(2,1)S(1)}, u32[]{:S(2)}, u32[]{:S(2)}) collective-permute-start(bf16[1296,128]{1,0:T(8,128)(2,1)S(1)} %collective-permute-done.9.refs_3_.refs_10_), channel_id=1, source_target_pairs={{0,1},{1,2},{2,3},{3,4},{4,5},{5,6},{6,7},{7,0},{8,9},{9,10},{10,1... | collective-permute-start | bytes 995336 | tf_op jit(solution)/shard_map/ppermute | solution.py:473
  66.1 9.6 %collective-permute-start.13 = (bf16[1296,128]{1,0:T(8,128)(2,1)S(1)}, bf16[1296,128]{1,0:T(8,128)(2,1)S(1)}, u32[]{:S(2)}, u32[]{:S(2)}) collective-permute-start(bf16[1296,128]{1,0:T(8,128)(2,1)S(1)} %collective-permute-done.11.refs_4_.refs_11_), channel_id=1, source_target_pairs={{0,7},{1,0},{2,1},{3,2},{4,3},{5,4},{6,5},{7,6},{8,15},{9,8},{10,9... | collective-permute-start | bytes 995336 | tf_op jit(solution)/shard_map/ppermute | solution.py:474
  75.6 8.2 %collective-permute-start.12 = (bf16[768,128]{1,0:T(8,128)(2,1)S(1)}, bf16[768,128]{1,0:T(8,128)(2,1)S(1)}, u32[]{:S(2)}, u32[]{:S(2)}) collective-permute-start(bf16[768,128]{1,0:T(8,128)(2,1)S(1)} %slice.14), channel_id=1, source_target_pairs={{0,1},{1,2},{2,3},{3,4},{4,5},{5,6},{6,7},{7,0},{8,9},{9,10},{10,1... | collective-permute-start | bytes 589832 | tf_op jit(solution)/shard_map/ppermute | solution.py:481
  75.7 8.1 %copy-start.2 = (bf16[16,512,128]{2,1,0:T(8,128)(2,1)S(1)}, bf16[16,512,128]{2,1,0:T(8,128)(2,1)}, u32[]{:S(2)}) copy-start(bf16[16,512,128]{2,1,0:T(8,128)(2,1)} %refs_14_.1) | copy-start | bytes 6291460
  75.8 8.1 %collective-permute-start.14 = (bf16[528,128]{1,0:T(8,128)(2,1)S(1)}, bf16[528,128]{1,0:T(8,128)(2,1)S(1)}, u32[]{:S(2)}, u32[]{:S(2)}) collective-permute-start(bf16[528,128]{1,0:T(8,128)(2,1)S(1)} %slice.16), channel_id=1, source_target_pairs={{0,7},{1,0},{2,1},{3,2},{4,3},{5,4},{6,5},{7,6},{8,15},{9,8},{10,9... | collective-permute-start | bytes 405512 | tf_op jit(solution)/shard_map/ppermute | solution.py:481
